TPU v7x, 128 devices: a whole 4x4x4 slice. The times are simulated.
128 devices in a mesh: gx: 16 (over z, x), gy: 4 (over y), af: 2 (over core).
Axes of the slice: x: 4, y: 4, z: 4, core: 2. Of those that a mesh axis runs over, the one named last changes fastest.
Arguments:
- fields: float32 [6, 512, 64, 256], P(None, 'gx', 'gy', 'af'), may hold values from -6 to 6
- polarization: float32 [2, 3, 512, 64, 256], P(None, None, 'gx', 'gy', 'af'), may hold values from -2 to 2
- material: int32 [512, 64, 256], P('gx', 'gy', 'af'), may hold values from 0 to 3
- eps_inf: float32 [4], replicated, may hold values from 1 to 4
- pole_strength: float32 [4], replicated, may hold values from 0.5 to 3
- pole_freq: float32 [4], replicated, may hold values from 0.4 to 1.2
- damping: float32 [4], replicated, may hold values from 0.05 to 1
- owner: int32 [4, 2, 64, 1], P('gy', 'af'), may hold values from 0 to 15; in each aligned block of 64 rows (0 to 63, 64 to 127, ..., all dimensions but the last counted through in order) at most 8 rows name the same one
Outputs:
- fields_next: float32 [6, 512, 64, 256], P(None, 'gx', 'gy', 'af')
- polarization_next: float32 [2, 3, 512, 64, 256], P(None, None, 'gx', 'gy', 'af')
- surface_spectra: float32 [16, 4, 2, 8, 64, 128], P('gx', 'gy', 'af')
- far_field: float32 [8, 4096], P(None, ('gx', 'gy', 'af'))
Inputs may be any that keep to these rules, and one draw needn't show every extreme that they name: `owner`: within the rows of one tile (aligned blocks of 64 rows) no gx index owns more than 8 rows, and some tile reaches 8.
All inputs are finite; a program needn't handle non-finite values.
Results may differ from a plain program's by a relative error of at most 0.0002.
Values sent between devices are 32-bit elements; how exact they have to be, the bound alone decides.
A program may use at most 128 MiB of HBM per device.

v0:
```python
import math

import jax
import jax.numpy as jnp
from jax import lax
from jax.sharding import PartitionSpec as P

STEPS = 8
NF = 32
NANG = 128
NMAT = 4


step_size = 0.5
HIGH = lax.Precision.HIGHEST


def extended(block, sides, width):
    for axis, dim in sides:
        count = lax.axis_size(axis)
        forward = [(i, i + 1) for i in range(count - 1)]
        backward = [(target, source) for source, target in forward]
        low = lax.ppermute(
            lax.slice_in_dim(block, block.shape[dim] - width, None, axis=dim), axis, forward
        )
        high = lax.ppermute(lax.slice_in_dim(block, 0, width, axis=dim), axis, backward)
        block = jnp.concatenate([low, block, high], axis=dim)
    return block


def coefficient_fields(material, eps_inf, pole_strength, pole_freq, damping):
    turning = pole_freq * step_size
    half_loss = damping * (0.5 * step_size)
    denominator = 1.0 + half_loss
    tables = [
        (2.0 - turning * turning) / denominator,
        -(1.0 - half_loss) / denominator,
        pole_strength * turning * turning / denominator,
        1.0 / eps_inf,
    ]
    fields_out = []
    for table_row in tables:
        values = jnp.zeros(material.shape, jnp.float32)
        for material_id in range(NMAT):
            values = jnp.where(material == material_id, table_row[material_id], values)
        fields_out.append(values)
    return fields_out


def frequencies():
    return 0.25 + 1.5 * jnp.arange(NF, dtype=jnp.float32) / NF


def time_table():
    phases = (jnp.arange(STEPS, dtype=jnp.float32) + 1.0) * step_size
    phases = phases[:, None] * frequencies()[None, :]
    return jnp.concatenate([jnp.cos(phases), -jnp.sin(phases)], axis=1) / STEPS


def directions():
    angles = jnp.arange(NANG, dtype=jnp.float32)
    bearing = 2.0 * math.pi * angles / NANG
    radius = 0.25 + 0.7 * (angles + 0.5) / NANG
    return (radius * jnp.cos(bearing), radius * jnp.sin(bearing))


def slot_table(owner_rows, owner_count, slot_count):
    one_hot = (owner_rows[..., None] == jnp.arange(owner_count, dtype=jnp.int32)).astype(jnp.int32)
    slot_rank = jnp.sum((jnp.cumsum(one_hot, axis=-2) - 1) * one_hot, axis=-1)
    chosen = (slot_rank[..., None] == jnp.arange(slot_count, dtype=jnp.int32)).astype(jnp.int32)
    picked = one_hot[..., :, :, None] * chosen[..., :, None, :]
    return jnp.moveaxis(picked, -3, -1).astype(jnp.float32)


def lower_mask(extent, position):
    return ((jnp.arange(extent) > 0) | (position > 0)).astype(jnp.float32)


def finish_update(state, current, previous, rates, curl, magnetic):
    keep_rate, back_rate, drive_rate, inverse_eps = rates
    electric = state[0:3]
    updated = keep_rate * current + back_rate * previous + drive_rate * electric
    electric = electric + inverse_eps * (step_size * curl - (updated - current))
    return (jnp.concatenate([electric, magnetic]), updated, current)


def advance(state, current, previous, rates, edge_mask):
    padded = extended(state, (("gx", 1), ("gy", 2), ("af", 3)), 1)
    size_x, size_y, size_z = (state.shape[1], state.shape[2], state.shape[3])
    region = (slice(0, size_x + 1), slice(0, size_y + 1), slice(0, size_z + 1))
    interior = (slice(1, size_x + 1), slice(1, size_y + 1), slice(1, size_z + 1))

    def ahead(values, spatial_dim):
        shifted = list(region)
        shifted[spatial_dim] = slice(1, values.shape[spatial_dim])
        return values[tuple(shifted)] - values[region]

    def behind(values, spatial_dim):
        shifted = list(interior)
        shifted[spatial_dim] = slice(0, values.shape[spatial_dim] - 1)
        return values[interior] - values[tuple(shifted)]

    electric_x, electric_y, electric_z = (padded[0], padded[1], padded[2])
    magnetic_x = (
        padded[3][region] - step_size * (ahead(electric_z, 1) - ahead(electric_y, 2))
    ) * edge_mask
    magnetic_y = (
        padded[4][region] - step_size * (ahead(electric_x, 2) - ahead(electric_z, 0))
    ) * edge_mask
    magnetic_z = (
        padded[5][region] - step_size * (ahead(electric_y, 0) - ahead(electric_x, 1))
    ) * edge_mask
    curl_x = behind(magnetic_z, 1) - behind(magnetic_y, 2)
    curl_y = behind(magnetic_x, 2) - behind(magnetic_z, 0)
    curl_z = behind(magnetic_y, 0) - behind(magnetic_x, 1)
    curl = jnp.stack([curl_x, curl_y, curl_z])
    magnetic = jnp.stack([magnetic_x[interior], magnetic_y[interior], magnetic_z[interior]])
    return finish_update(state, current, previous, rates, curl, magnetic)


def on_device(fields, polarization, material, eps_inf, pole_strength, pole_freq, damping, owner):
    rates = coefficient_fields(material, eps_inf, pole_strength, pole_freq, damping)
    cell_x, cell_y, cell_z = material.shape
    gx_count = lax.axis_size("gx")
    slot_count = 8 * cell_y // gx_count
    row_count = 4 * cell_y
    picked = slot_table(owner.reshape(row_count), gx_count, slot_count)
    holder = gx_count - 1
    monitor_x = cell_x - cell_x // 2
    holder_flag = (lax.axis_index("gx") == holder).astype(jnp.float32)
    edge_mask = (
        lower_mask(cell_x + 1, lax.axis_index("gx"))[:, None, None]
        * lower_mask(cell_y + 1, lax.axis_index("gy"))[None, :, None]
        * lower_mask(cell_z + 1, lax.axis_index("af"))[None, None, :]
    )
    time_weights = time_table()
    state = fields
    current = polarization[0]
    previous = polarization[1]
    collected = jnp.zeros((row_count, 2 * NF, cell_z), jnp.float32)
    for step_number in range(STEPS):
        state, current, previous = advance(state, current, previous, rates, edge_mask)
        samples = jnp.stack(
            [state[1, monitor_x], state[2, monitor_x], state[4, monitor_x], state[5, monitor_x]]
        )
        samples = samples.reshape(row_count, cell_z) * holder_flag
        weights_now = time_weights[step_number]
        collected = collected + weights_now[None, :, None] * samples[:, None, :]
    outgoing = jnp.einsum("osr,rkz->oskz", picked, collected, precision=HIGH)
    collected = lax.all_to_all(outgoing, "gx", split_axis=0, concat_axis=0, tiled=True)[holder]
    own_picks = lax.dynamic_index_in_dim(picked, lax.axis_index("gx"), 0, keepdims=False)
    slot_row = jnp.sum(
        own_picks * jnp.arange(row_count, dtype=jnp.float32)[None, :], axis=1
    ).astype(jnp.int32)
    occupied = jnp.sum(own_picks, axis=1)
    component = slot_row // cell_y
    y_local = slot_row % cell_y
    component_hot = (component[None, :] == jnp.arange(4, dtype=jnp.int32)[:, None]).astype(
        jnp.float32
    ) * occupied[None, :]
    y_slot = (lax.axis_index("gy") * cell_y + y_local).astype(jnp.float32)
    omegas = frequencies()
    along_y, along_z = directions()
    z_values = (lax.axis_index("af") * cell_z + jnp.arange(cell_z, dtype=jnp.int32)).astype(
        jnp.float32
    )
    z_phase = omegas[:, None, None] * along_z[None, None, :] * z_values[None, :, None]
    cos_z = jnp.cos(z_phase)
    sin_z = jnp.sin(z_phase)
    real_part = collected[:, :NF]
    imag_part = collected[:, NF:]
    inner_real = jnp.einsum("sfz,fza->sfa", real_part, cos_z, precision=HIGH) - jnp.einsum(
        "sfz,fza->sfa", imag_part, sin_z, precision=HIGH
    )
    inner_imag = jnp.einsum("sfz,fza->sfa", real_part, sin_z, precision=HIGH) + jnp.einsum(
        "sfz,fza->sfa", imag_part, cos_z, precision=HIGH
    )
    y_phase = omegas[None, :, None] * along_y[None, None, :] * y_slot[:, None, None]
    cos_y = jnp.cos(y_phase)
    sin_y = jnp.sin(y_phase)
    far_real = jnp.einsum(
        "cs,sfa->cfa", component_hot, inner_real * cos_y - inner_imag * sin_y, precision=HIGH
    )
    far_imag = jnp.einsum(
        "cs,sfa->cfa", component_hot, inner_real * sin_y + inner_imag * cos_y, precision=HIGH
    )
    far_scale = 1.0 / math.sqrt(cell_y * lax.axis_size("gy") * cell_z * lax.axis_size("af"))
    partial_far = jnp.stack([far_real, far_imag], axis=1).reshape(8, NF * NANG) * far_scale
    far_field = lax.psum_scatter(partial_far, ("gx", "gy", "af"), scatter_dimension=1, tiled=True)
    return (state, jnp.stack([current, previous]), collected[None, None, None], far_field)


def solution(mesh):
    return jax.shard_map(
        on_device,
        mesh=mesh,
        in_specs=(
            P(None, "gx", "gy", "af"),
            P(None, None, "gx", "gy", "af"),
            P("gx", "gy", "af"),
            P(),
            P(),
            P(),
            P(),
            P("gy", "af", None, None),
        ),
        out_specs=(
            P(None, "gx", "gy", "af"),
            P(None, None, "gx", "gy", "af"),
            P("gx", "gy", "af", None, None, None),
            P(None, ("gx", "gy", "af")),
        ),
        check_vma=False,
    )
```

profile of v0, /device:TPU:1, one launch (start us, length us, event | category | flops | bytes accessed | tf_op | source)
XLA Modules:
  0.0 1199.5 jit_solution(637621523221825130)
XLA Ops:
  9.3 4.6 collective-permute-start
  20.8 3.7 select_select_fusion.3
  24.5 7.7 select_select_fusion.2
  33.4 3.4 collective-permute-start.2
  38.8 3.5 collective-permute-done.3
  50.3 5.2 collective-permute-start.5
  64.3 5.3 pad_maximum_fusion
  77.8 3.5 collective-permute-done.7
  100.5 5.5 collective-permute-start.11
  116.3 8.7 pad_maximum_fusion.1
  128.8 4.4 collective-permute-start.12
  134.5 3.8 collective-permute-done.13
  143.1 3.8 collective-permute-done.15
  155.4 5.4 collective-permute-start.17
  169.1 8.6 pad_maximum_fusion.2
  180.6 3.7 collective-permute-start.18
  185.7 3.8 collective-permute-done.19
  193.1 3.7 collective-permute-done.21
  206.6 5.3 collective-permute-start.23
  222.1 8.7 pad_maximum_fusion.3
  234.3 3.7 collective-permute-start.24
  239.4 3.8 collective-permute-done.25
  246.7 3.8 collective-permute-done.27
  259.0 4.7 collective-permute-start.29
  272.1 8.6 pad_maximum_fusion.4
  283.6 3.7 collective-permute-start.30
  288.7 3.8 collective-permute-done.31
  296.0 3.8 collective-permute-done.33
  309.6 5.3 collective-permute-start.35
  325.1 8.7 pad_maximum_fusion.5
  337.3 3.7 collective-permute-start.36
  342.4 3.8 collective-permute-done.37
  349.7 3.7 collective-permute-done.39
  362.0 4.7 collective-permute-start.41
  375.1 8.6 pad_maximum_fusion.6
  387.6 3.7 collective-permute-start.42
  392.7 3.8 collective-permute-done.43
  399.9 3.8 collective-permute-done.45
  413.5 5.3 collective-permute-start.47
  429.1 8.7 pad_maximum_fusion.7
  442.2 6.2 fusion.4
  448.4 9.4 all-to-all-start
  458.7 62.0 %all-to-all-done = f32[16,8,64,128]{3,1,2,0:T(8,128)} async-done(((f32[16,8,64,128]{3,1,2,0:T(8,128)}), f32[16,8,64,128]{3,1,2,0:T(8,128)}, u32[]{:S(2)}, u32[]{:S(2)}) %all-to-all-start) | async-done | bytes 4194336 | tf_op jit(solution)/shard_map/all_to_all | solution.py:150
  521.7 8.6 fusion
  530.3 8.8 fusion.1
  539.1 8.9 fusion.24
  548.0 8.7 fusion.22
  564.3 626.8 %reduce-scatter.4.cloned.1.call-done = f32[32,8]{1,0:T(8,128)} async-done(((f32[4096,8]{1,0:T(8,128)}), f32[32,8]{1,0:T(8,128)}) %reduce-scatter.4.cloned.1.call-update) | async-done | bytes 1040
  (420 shorter events, 241.9 us)
Async XLA Ops:
  8.0 25.2 %collective-permute-start.1 = (f32[6,1,16,128]{3,2,1,0:T(8,128)S(1)}, f32[6,1,16,128]{3,2,1,0:T(8,128)S(1)}, u32[]{:S(2)}, u32[]{:S(2)}) collective-permute-start(f32[6,1,16,128]{3,2,1,0:T(8,128)S(1)} %get-tuple-element.140), channel_id=1, source_target_pairs={{8,0},{16,8},{24,16},{32,24},{40,32},{48,40},{56,48},{64,56},{72,6... | collective-permute-start | bytes 147464 | tf_op jit(solution)/shard_map/ppermute | solution.py:26
  9.3 23.8 %collective-permute-start = (f32[6,1,16,128]{3,2,1,0:T(8,128)S(1)}, f32[6,1,16,128]{3,2,1,0:T(8,128)S(1)}, u32[]{:S(2)}, u32[]{:S(2)}) collective-permute-start(f32[6,1,16,128]{3,2,1,0:T(8,128)S(1)} %get-tuple-element.141), channel_id=1, source_target_pairs={{0,8},{8,16},{16,24},{24,32},{32,40},{40,48},{48,56},{56,64},{64,7... | collective-permute-start | bytes 147464 | tf_op jit(solution)/shard_map/ppermute | solution.py:23
  33.4 5.4 collective-permute-start.2
  36.9 5.4 collective-permute-start.3
  50.3 10.6 collective-permute-start.5
  55.5 3.5 collective-permute-start.4
  73.4 4.4 collective-permute-start.6
  76.5 4.8 collective-permute-start.7
  81.5 5.3 collective-permute-start.8
  84.7 5.4 collective-permute-start.9
  100.5 12.4 %collective-permute-start.11 = (f32[6,34,18,1]{1,3,2,0:T(1,128)}, f32[6,34,18,1]{1,3,2,0:T(1,128)}, u32[]{:S(2)}, u32[]{:S(2)}) collective-permute-start(f32[6,34,18,1]{1,3,2,0:T(1,128)} %copy.108), channel_id=1, source_target_pairs={{1,0},{3,2},{5,4},{7,6},{9,8},{11,10},{13,12},{15,14},{17,16},{19,... | collective-permute-start | bytes 44072 | tf_op jit(solution)/shard_map/ppermute | solution.py:26
  106.1 3.5 collective-permute-start.10
  128.8 5.7 collective-permute-start.12
  133.2 5.1 collective-permute-start.13
  138.5 4.6 collective-permute-start.14
  141.4 5.4 collective-permute-start.15
  155.4 11.1 collective-permute-start.17
  160.8 3.1 collective-permute-start.16
  180.6 5.1 collective-permute-start.18
  184.4 5.1 collective-permute-start.19
  189.7 3.4 collective-permute-start.20
  191.3 5.4 collective-permute-start.21
  206.6 12.2 %collective-permute-start.23 = (f32[6,34,18,1]{1,3,2,0:T(1,128)}, f32[6,34,18,1]{1,3,2,0:T(1,128)}, u32[]{:S(2)}, u32[]{:S(2)}) collective-permute-start(f32[6,34,18,1]{1,3,2,0:T(1,128)} %copy.116), channel_id=1, source_target_pairs={{1,0},{3,2},{5,4},{7,6},{9,8},{11,10},{13,12},{15,14},{17,16},{19,... | collective-permute-start | bytes 44072 | tf_op jit(solution)/shard_map/ppermute | solution.py:26
  211.9 3.5 collective-permute-start.22
  234.3 5.1 collective-permute-start.24
  238.1 5.1 collective-permute-start.25
  243.4 3.3 collective-permute-start.26
  245.0 5.4 collective-permute-start.27
  259.0 10.4 collective-permute-start.29
  283.6 5.1 collective-permute-start.30
  287.4 5.1 collective-permute-start.31
  292.7 3.3 collective-permute-start.32
  294.3 5.4 collective-permute-start.33
  309.6 12.2 %collective-permute-start.35 = (f32[6,34,18,1]{1,3,2,0:T(1,128)}, f32[6,34,18,1]{1,3,2,0:T(1,128)}, u32[]{:S(2)}, u32[]{:S(2)}) collective-permute-start(f32[6,34,18,1]{1,3,2,0:T(1,128)} %copy.124), channel_id=1, source_target_pairs={{1,0},{3,2},{5,4},{7,6},{9,8},{11,10},{13,12},{15,14},{17,16},{19,... | collective-permute-start | bytes 44072 | tf_op jit(solution)/shard_map/ppermute | solution.py:26
  314.8 3.5 collective-permute-start.34
  337.3 5.1 collective-permute-start.36
  341.1 5.1 collective-permute-start.37
  346.4 3.4 collective-permute-start.38
  348.0 5.4 collective-permute-start.39
  362.0 10.5 collective-permute-start.41
  387.6 5.1 collective-permute-start.42
  391.3 5.1 collective-permute-start.43
  396.6 3.3 collective-permute-start.44
  398.3 5.4 collective-permute-start.45
  413.5 12.2 %collective-permute-start.47 = (f32[6,34,18,1]{1,3,2,0:T(1,128)}, f32[6,34,18,1]{1,3,2,0:T(1,128)}, u32[]{:S(2)}, u32[]{:S(2)}) collective-permute-start(f32[6,34,18,1]{1,3,2,0:T(1,128)} %copy.132), channel_id=1, source_target_pairs={{1,0},{3,2},{5,4},{7,6},{9,8},{11,10},{13,12},{15,14},{17,16},{19,... | collective-permute-start | bytes 44072 | tf_op jit(solution)/shard_map/ppermute | solution.py:26
  418.8 3.5 collective-permute-start.46
  448.4 72.3 %all-to-all-start = ((f32[16,8,64,128]{3,1,2,0:T(8,128)}), f32[16,8,64,128]{3,1,2,0:T(8,128)}, u32[]{:S(2)}, u32[]{:S(2)}) async-start(f32[16,8,64,128]{3,1,2,0:T(8,128)} %fusion.4), calls=%async_computation | async-start | bytes 8388608 | tf_op jit(solution)/shard_map/all_to_all | solution.py:150
  457.8 733.2 %reduce-scatter.4.cloned.1.call-start = ((), (), s32[]{:S(2)}) async-start(), calls=%async_computation.2 | async-start | bytes 2113536
  (94 other events, 758.9 us)
Sparse Core Ops, SparseCore 0:
  560.5 630.5 reduce-scatter.3
where the time goes:
time: 1220 us; the launch traced here: 1200 us
  waiting for transfers between devices  756 us (62%)
  local copies, waits for them, and re-layouts  139 us (11%)
  starting transfers between devices  133 us (11%)
  other arithmetic  114 us (9%)
  matrix products  42.7 us (4%)
  between operations  16.1 us (1%)
    unnamed x2, waiting for transfers between devices  627 us
    concatenate x16, other arithmetic, extended(): block = jnp.concatenate([low, block, high], axis=dim)  69.3 us
    ppermute x24, starting transfers between devices, extended(): lax.ppermute(lax.slice_in_dim(block, 0, width, axis=dim), axis, backward)  63.8 us
    all_to_all x1, waiting for transfers between devices, on_device(): lax.all_to_all(outgoing, 'gx', split_axis=0, concat_axis=0, tiled=True)  62 us
    ppermute x24, starting transfers between devices, extended(): lax.ppermute(lax.slice_in_dim(block, block.shape[dim] - width, None, axis...  58.9 us
    ppermute x24, waiting for transfers between devices, extended(): lax.ppermute(lax.slice_in_dim(block, 0, width, axis=dim), axis, backward)  55.6 us
    slice x17, local copies, waits for them, and re-layouts, extended(): lax.slice_in_dim(block, block.shape[dim] - width, None, axis=dim)  47.1 us
    ppermute x8, local copies, waits for them, and re-layouts, extended(): lax.ppermute(lax.slice_in_dim(block, 0, width, axis=dim), axis, backward)  24.8 us
  transfers between devices with their start and end apart: 50, of which 29 were waited for; matrix products, arithmetic and copies ran while one was open for 4% of the time, Pallas kernels for 0%

commit v1 on v0

v1 whole, which is shorter than its diff:
```python
import functools
import math

import jax
import jax.numpy as jnp
import numpy as np
from jax import lax
from jax.experimental import pallas as pl
from jax.experimental.pallas import tpu as pltpu
from jax.sharding import PartitionSpec as P

STEPS = 8
NF = 32
NANG = 128
NMAT = 4
NGX, NGY, NAF = 16, 4, 2
BX, BY, BZ = 32, 16, 128
HX = BX // 2
SLOTS = 8
DT = 0.5
MESH = pl.DeviceIdType.MESH
HIGHEST = lax.Precision.HIGHEST
F32 = jnp.float32


def tables():
    omega = 0.25 + 1.5 * np.arange(NF) / NF
    t = (np.arange(STEPS) + 1.0) * DT
    phase = t[:, None] * omega[None, :]
    weights = np.concatenate([np.cos(phase), -np.sin(phase)], axis=1) / STEPS
    angle = np.arange(NANG)
    rho = 0.25 + 0.7 * (angle + 0.5) / NANG
    s_y = rho * np.cos(2.0 * np.pi * angle / NANG)
    s_z = rho * np.sin(2.0 * np.pi * angle / NANG)
    z_phase = omega[:, None, None] * s_z[None, None, :] * np.arange(BZ)[None, :, None]
    z_table = np.concatenate([np.cos(z_phase), np.sin(z_phase)], axis=2)
    z_table = z_table.reshape(NGX, 2, BZ, 2 * NANG)
    y = np.arange(NGY * BY).reshape(NGY, 1, BY)
    z0 = (BZ * np.arange(NAF)).reshape(1, NAF, 1)
    shift = s_y * y[..., None] + s_z * z0[..., None]
    y_phase = omega[:, None, None] * shift[:, :, None]
    y_table = np.stack([np.cos(y_phase), np.sin(y_phase)], axis=3)
    y_table = y_table / math.sqrt(NGY * BY * NAF * BZ)
    y_table = y_table.reshape(NGY * NAF, NGX, 2, 2, BY, NANG)
    spread = np.broadcast_to(weights[:, :, None], (STEPS, 2 * NF, 128))
    return (
        weights.astype(np.float32),
        spread.astype(np.float32),
        z_table.astype(np.float32),
        y_table.astype(np.float32),
    )


def kernel(
    eps_ref, strength_ref, freq_ref, damp_ref, weight_ref, owner_ref,
    fields_ref, pol_ref, mat_ref, spread_hbm, ztab_hbm, ytab_hbm,
    out_f, out_p, out_s, out_far,
    E, H, PQ, mat, coef, stage, samp, ztab, ytab, spread, part, parts,
    local_sem, swap_send, swap_recv, halo_send, halo_recv, first_send, first_recv,
    samp_send, samp_recv, far_send, far_recv, out_sem, out_send, out_recv,
):
    gx, gy, c = lax.axis_index("gx"), lax.axis_index("gy"), lax.axis_index("af")
    place = 2 * gx + c
    other = 1 - c
    has_up, has_down = place < 2 * NGX - 1, place > 0
    has_right, has_left = gy < NGY - 1, gy > 0
    up = (gx + c, gy, other)
    down = (gx - other, gy, other)
    right, left = (gx, gy + 1, c), (gx, gy - 1, c)
    up_left = (gx + c, gy - 1, other)
    down_right = (gx - other, gy + 1, other)
    partner = (gx, gy, other)
    is_holder = jnp.logical_and(gx == NGX - 1, c == 1)
    me = gy * NAF + c

    barrier = pltpu.get_barrier_semaphore()

    def greet(device):
        pl.semaphore_signal(barrier, inc=1, device_id=device, device_id_type=MESH)

    for k in range(1, NGY * NAF):
        them = lax.rem(me + k, NGY * NAF)
        greet((gx, them // NAF, lax.rem(them, NAF)))
    across_up = jnp.logical_and(c == 1, has_up)
    across_down = jnp.logical_and(c == 0, has_down)
    across_up_left = jnp.logical_and(across_up, has_left)
    across_down_right = jnp.logical_and(across_down, has_right)
    for there, device in (
        (across_up, up), (across_down, down), (across_up_left, up_left), (across_down_right, down_right),
    ):
        @pl.when(there)
        def _(device=device):
            greet(device)

    @pl.when(jnp.logical_not(is_holder))
    def _():
        greet((NGX - 1, gy, 1))

    here = pl.ds(c * HX, HX)
    there = pl.ds(other * HX, HX)
    loads = [
        (fields_ref.at[0:3, here], E.at[0, :, c, 1:HX + 1, 8:24]),
        (fields_ref.at[3:6, here], H.at[:, c, 1:HX + 1, 8:24]),
        (pol_ref.at[:, :, here], PQ.at[:, :, c]),
        (mat_ref.at[here], mat.at[c]),
        (ztab_hbm.at[gx], ztab),
        (ytab_hbm.at[me, gx], ytab),
        (spread_hbm, spread),
    ]
    loads = [pltpu.make_async_copy(s, d, local_sem.at[i]) for i, (s, d) in enumerate(loads)]
    for copy in loads:
        copy.start()

    @pl.when(jnp.logical_not(has_up))
    def _():
        for p in range(2):
            for d in (1, 2):
                for z in range(2):
                    E[p, d, z, HX + 1, 0:24] = jnp.zeros((24, 128), F32)

    @pl.when(jnp.logical_not(has_right))
    def _():
        @pl.loop(0, HX + 1)
        def _(i):
            for p in range(2):
                for d in (0, 2):
                    for z in range(2):
                        E[p, d, z, i, 24:32] = jnp.zeros((8, 128), F32)

    count = (
        NGY * NAF - 1
        + across_up.astype(jnp.int32) + across_down.astype(jnp.int32)
        + across_up_left.astype(jnp.int32) + across_down_right.astype(jnp.int32)
        + jnp.where(is_holder, 2 * NGX - 1, 0)
    )
    pl.semaphore_wait(barrier, count)

    swaps = [
        (fields_ref.at[0:3, there], E.at[0, :, c, 1:HX + 1, 8:24]),
        (fields_ref.at[3:6, there], H.at[:, c, 1:HX + 1, 8:24]),
        (pol_ref.at[:, :, there], PQ.at[:, :, c]),
        (mat_ref.at[there], mat.at[c]),
    ]
    swaps = [
        pltpu.make_async_remote_copy(
            src_ref=s, dst_ref=d, send_sem=swap_send.at[i], recv_sem=swap_recv.at[i],
            device_id=partner, device_id_type=MESH,
        )
        for i, (s, d) in enumerate(swaps)
    ]
    for copy in swaps:
        copy.start()
    for i in range(2):
        loads[i].wait()
        swaps[i].wait()

    def halos(p):
        def message(k, src, dst, device):
            return pltpu.make_async_remote_copy(
                src_ref=src, dst_ref=dst, send_sem=halo_send.at[k], recv_sem=halo_recv.at[p, k],
                device_id=device, device_id_type=MESH,
            )

        own, rows = pl.ds(1, HX), pl.ds(8, BY)
        return [
            (has_up, has_down, message(0, E.at[p, :, :, HX, rows], E.at[p, :, :, 0, rows], up)),
            (has_down, has_up, message(1, E.at[p, 1:3, :, 1, rows], E.at[p, 1:3, :, HX + 1, rows], down)),
            (has_right, has_left, message(2, E.at[p, :, :, own, 23:24], E.at[p, :, :, own, 7:8], right)),
            (has_left, has_right, message(3, E.at[p, 0, :, own, 8:9], E.at[p, 0, :, own, 24:25], left)),
            (has_left, has_right, message(4, E.at[p, 2, :, own, 8:9], E.at[p, 2, :, own, 24:25], left)),
            (
                jnp.logical_and(has_up, has_left), jnp.logical_and(has_down, has_right),
                message(5, E.at[p, 0, :, HX, 8:9], E.at[p, 0, :, 0, 24:25], up_left),
            ),
            (
                jnp.logical_and(has_down, has_right), jnp.logical_and(has_up, has_left),
                message(6, E.at[p, 1, :, 1, 23:24], E.at[p, 1, :, HX + 1, 7:8], down_right),
            ),
        ]

    def start(messages):
        for receiver, _, copy in messages:
            @pl.when(receiver)
            def _(copy=copy):
                copy.start()

    def finish(messages):
        for receiver, sender, copy in messages:
            @pl.when(sender)
            def _(copy=copy):
                copy.wait_recv()

            @pl.when(receiver)
            def _(copy=copy):
                copy.wait_send()

    def first(k, src, dst, device):
        return pltpu.make_async_remote_copy(
            src_ref=src, dst_ref=dst, send_sem=first_send.at[k], recv_sem=first_recv.at[k],
            device_id=device, device_id_type=MESH,
        )

    own, rows = pl.ds(1, HX), pl.ds(8, BY)
    h_layers = [
        (has_up, has_down, first(0, H.at[1:3, :, HX, rows], H.at[1:3, :, 0, rows], up)),
        (has_right, has_left, first(1, H.at[0, :, own, 23:24], H.at[0, :, own, 7:8], right)),
        (has_right, has_left, first(2, H.at[2, :, own, 23:24], H.at[2, :, own, 7:8], right)),
    ]
    start(h_layers)
    start(halos(0))
    for i in range(2, 4):
        loads[i].wait()
        swaps[i].wait()
    for copy in loads[4:]:
        copy.wait()

    rates = [[], [], [], []]
    for m in range(NMAT):
        turning = jnp.full((8, 128), freq_ref[m], F32) * DT
        half_loss = jnp.full((8, 128), damp_ref[m], F32) * (0.5 * DT)
        denominator = 1.0 + half_loss
        rates[0].append((2.0 - turning * turning) / denominator)
        rates[1].append(-(1.0 - half_loss) / denominator)
        rates[2].append(jnp.full((8, 128), strength_ref[m], F32) * turning * turning / denominator)
        rates[3].append(1.0 / jnp.full((8, 128), eps_ref[m], F32))

    @pl.loop(0, HX)
    def _(i):
        for z in range(2):
            for j in range(2):
                cell = mat[z, i, 8 * j:8 * j + 8]
                for k in range(4):
                    value = jnp.where(cell == 1, rates[k][1], rates[k][0])
                    value = jnp.where(cell == 2, rates[k][2], value)
                    coef[k, z, i, 8 * j:8 * j + 8] = jnp.where(cell == 3, rates[k][3], value)

    finish(h_layers)

    lane = lax.broadcasted_iota(jnp.int32, (8, 128), 1)
    last_lane, first_lane = lane == 127, lane == 0

    def ahead_z(v):
        r0, r1 = (pltpu.roll(x, 127, 1) for x in v)
        return jnp.where(last_lane, r1, r0), jnp.where(last_lane, 0.0, r1)

    def behind_z(v):
        r0, r1 = (pltpu.roll(x, 1, 1) for x in v)
        return jnp.where(first_lane, 0.0, r0), jnp.where(first_lane, r0, r1)

    def magnetic(p, i, j, keep):
        r = pl.ds(8 * j, 8)
        r1 = pl.ds(8 * j + 1, 8)
        ex, ey, ez = ([E[p, d, z, i, r] for z in range(2)] for d in range(3))
        ex_z, ey_z = ahead_z(ex), ahead_z(ey)
        for z in range(2):
            hx = H[0, z, i, r] - DT * ((E[p, 2, z, i, r1] - ez[z]) - (ey_z[z] - ey[z]))
            hy = H[1, z, i, r] - DT * ((ex_z[z] - ex[z]) - (E[p, 2, z, i + 1, r] - ez[z]))
            hz = H[2, z, i, r] - DT * ((E[p, 1, z, i + 1, r] - ey[z]) - (E[p, 0, z, i, r1] - ex[z]))
            if keep is not None:
                hx, hy, hz = (jnp.where(keep, h, 0.0) for h in (hx, hy, hz))
            H[0, z, i, r] = hx
            H[1, z, i, r] = hy
            H[2, z, i, r] = hz

    def electric(p, i, j):
        q = 1 - p
        r = pl.ds(8 * j, 8)
        r1 = pl.ds(8 * j - 1, 8)
        s = pl.ds(8 * (j - 1), 8)
        hx, hy, hz = ([H[d, z, i, r] for z in range(2)] for d in range(3))
        hx_z, hy_z = behind_z(hx), behind_z(hy)
        for z in range(2):
            curl = (
                (hz[z] - H[2, z, i, r1]) - (hy[z] - hy_z[z]),
                (hx[z] - hx_z[z]) - (hz[z] - H[2, z, i - 1, r]),
                (hy[z] - H[1, z, i - 1, r]) - (hx[z] - H[0, z, i, r1]),
            )
            keep, back, drive, inverse = (coef[k, z, i - 1, s] for k in range(4))
            for d in range(3):
                e = E[p, d, z, i, r]
                now = PQ[p, d, z, i - 1, s]
                new = keep * now + back * PQ[q, d, z, i - 1, s] + drive * e
                PQ[q, d, z, i - 1, s] = new
                E[q, d, z, i, r] = e + inverse * (DT * curl[d] - (new - now))

    def sample_copy(n, g, t):
        return pltpu.make_async_remote_copy(
            src_ref=stage.at[n, t], dst_ref=samp.at[n], send_sem=samp_send.at[g, t], recv_sem=samp_recv.at[n],
            device_id=(g, gy, t), device_id_type=MESH,
        )

    def each_receiver(act):
        @pl.loop(0, NGX)
        def _(g):
            act(g, 0)

            @pl.when(g < NGX - 1)
            def _():
                act(g, 1)

    @pl.loop(0, STEPS)
    def _(n):
        p = lax.rem(n, 2)

        @pl.when(n > 0)
        def _():
            start(halos(p))

        finish(halos(p))
        magnetic(p, 0, 1, has_down)
        magnetic(p, 0, 2, has_down)

        @pl.loop(1, HX + 1)
        def _(i):
            magnetic(p, i, 0, has_left)
            magnetic(p, i, 1, None)
            magnetic(p, i, 2, None)

        @pl.loop(1, HX + 1)
        def _(i):
            electric(p, i, 1)
            electric(p, i, 2)

        @pl.when(is_holder)
        def _():
            @pl.when(n > 0)
            def _():
                each_receiver(lambda g, t: sample_copy(n - 1, g, t).wait_send())

            for t in range(2):
                for d in range(2):
                    stage[n, t, d] = E[1 - p, d + 1, t, 1, 8:24]
                    stage[n, t, d + 2] = H[d + 1, t, 1, 8:24]
            each_receiver(lambda g, t: sample_copy(n, g, t).start())
            samp[n] = stage[n, 1]

    e_out = lambda z: (E.at[0, :, z, own, rows], out_f.at[0:3, here])
    h_out = lambda z: (H.at[:, z, own, rows], out_f.at[3:6, here])
    p_out = lambda z: (PQ.at[:, :, z], out_p.at[:, :, here])
    sends = []
    for k, out in enumerate((e_out, h_out, p_out)):
        s, d = out(other)
        sends.append(pltpu.make_async_remote_copy(
            src_ref=s, dst_ref=d, send_sem=out_send.at[k], recv_sem=out_recv.at[k],
            device_id=partner, device_id_type=MESH,
        ))
        s, d = out(c)
        sends.append(pltpu.make_async_copy(s, d, out_sem.at[k]))
    for copy in sends:
        copy.start()

    @pl.when(is_holder)
    def _():
        each_receiver(lambda g, t: sample_copy(STEPS - 1, g, t).wait_send())

    @pl.when(jnp.logical_not(is_holder))
    def _():
        for n in range(STEPS):
            sample_copy(n, 0, 0).wait_recv()

    rows_of = [samp[n].reshape(4 * BY, 128) for n in range(STEPS)]
    for f in range(2):
        real = weight_ref[0, 2 * gx + f] * rows_of[0]
        imag = weight_ref[0, NF + 2 * gx + f] * rows_of[0]
        for n in range(1, STEPS):
            real += weight_ref[n, 2 * gx + f] * rows_of[n]
            imag += weight_ref[n, NF + 2 * gx + f] * rows_of[n]
        both = jnp.concatenate([real, imag], axis=0)
        inner = jnp.dot(both, ztab[f], precision=HIGHEST, preferred_element_type=F32)
        inner_real = inner[:64, :128] - inner[64:, 128:]
        inner_imag = inner[:64, 128:] + inner[64:, :128]
        cos_y, sin_y = ytab[f, 0], ytab[f, 1]
        lines = []
        for d in range(4):
            re, im = inner_real[16 * d:16 * d + 16], inner_imag[16 * d:16 * d + 16]
            lines.append(jnp.sum(re * cos_y - im * sin_y, axis=0, keepdims=True))
            lines.append(jnp.sum(re * sin_y + im * cos_y, axis=0, keepdims=True))
        part[f] = jnp.concatenate(lines, axis=0)

    far = []
    for k in range(1, NGY * NAF):
        them = lax.rem(me + k, NGY * NAF)
        far.append(pltpu.make_async_remote_copy(
            src_ref=part.at[them // 4], dst_ref=parts.at[k], send_sem=far_send.at[k], recv_sem=far_recv.at[k],
            device_id=(gx, them // NAF, lax.rem(them, NAF)), device_id_type=MESH,
        ))
    for copy in far:
        copy.start()

    mine = (owner_ref[...] == gx).astype(F32)
    row = lax.broadcasted_iota(jnp.int32, (64, 64), 0)
    col = lax.broadcasted_iota(jnp.int32, (64, 64), 1)
    rank = jnp.dot((col < row).astype(F32), mine, precision=HIGHEST, preferred_element_type=F32)
    slot = lax.broadcasted_iota(jnp.int32, (64, 128), 1).astype(F32)
    picked = jnp.where(rank == slot, mine, 0.0)
    chosen = [
        lax.dot_general(picked, rows_of[n], (((0,), (0,)), ((), ())), precision=HIGHEST, preferred_element_type=F32)
        for n in range(STEPS)
    ]
    for s in range(SLOTS):
        for k in range(2 * NF // 8):
            total = spread[0, 8 * k:8 * k + 8] * chosen[0][s:s + 1]
            for n in range(1, STEPS):
                total += spread[n, 8 * k:8 * k + 8] * chosen[n][s:s + 1]
            out_s[0, 0, 0, s, 8 * k:8 * k + 8] = total

    total = part[me // 4]
    for k in range(1, NGY * NAF):
        far[k - 1].wait()
        total += parts[k]
    block = lax.rem(me, 4)
    total = pltpu.roll(total, lax.rem(128 - 32 * block, 128), 1)
    out_far[...] = total[:, :32]
    for copy in sends:
        copy.wait()


def on_device(constants, fields, polarization, material, eps_inf, pole_strength, pole_freq, damping, owner):
    weights, spread, z_table, y_table = constants
    smem = pl.BlockSpec(memory_space=pltpu.SMEM)
    vmem = pl.BlockSpec(memory_space=pltpu.VMEM)
    hbm = pl.BlockSpec(memory_space=pl.ANY)
    dma = lambda *shape: pltpu.SemaphoreType.DMA(shape)
    return pl.pallas_call(
        kernel,
        out_shape=(
            jax.ShapeDtypeStruct(fields.shape, F32),
            jax.ShapeDtypeStruct(polarization.shape, F32),
            jax.ShapeDtypeStruct((1, 1, 1, SLOTS, 2 * NF, BZ), F32),
            jax.ShapeDtypeStruct((8, 32), F32),
        ),
        in_specs=[smem] * 5 + [vmem] + [hbm] * 6,
        out_specs=(hbm, hbm, vmem, vmem),
        scratch_shapes=[
            pltpu.VMEM((2, 3, 2, HX + 2, 32, 128), F32),
            pltpu.VMEM((3, 2, HX + 1, 24, 128), F32),
            pltpu.VMEM((2, 3, 2, HX, BY, 128), F32),
            pltpu.VMEM((2, HX, BY, 128), jnp.int32),
            pltpu.VMEM((4, 2, HX, BY, 128), F32),
            pltpu.VMEM((STEPS, 2, 4, BY, 128), F32),
            pltpu.VMEM((STEPS, 4, BY, 128), F32),
            pltpu.VMEM((2, BZ, 2 * NANG), F32),
            pltpu.VMEM((2, 2, BY, NANG), F32),
            pltpu.VMEM((STEPS, 2 * NF, 128), F32),
            pltpu.VMEM((2, 8, 128), F32),
            pltpu.VMEM((8, 8, 128), F32),
            dma(7), dma(4), dma(4), dma(7), dma(2, 7), dma(3), dma(3),
            dma(NGX, 2), dma(STEPS), dma(8), dma(8), dma(3), dma(3), dma(3),
        ],
        compiler_params=pltpu.CompilerParams(
            collective_id=0, has_side_effects=True, vmem_limit_bytes=56 << 20
        ),
        name="fdtd",
    )(
        eps_inf, pole_strength, pole_freq, damping, weights, owner.reshape(64, 1),
        fields, polarization, material, spread, z_table, y_table,
    )


def solution(mesh):
    constants = tables()

    def whole(*arguments):
        return on_device(tuple(jnp.asarray(x) for x in constants), *arguments)

    return jax.shard_map(
        whole,
        mesh=mesh,
        in_specs=(
            P(None, "gx", "gy", "af"),
            P(None, None, "gx", "gy", "af"),
            P("gx", "gy", "af"),
            P(), P(), P(), P(),
            P("gy", "af", None, None),
        ),
        out_specs=(
            P(None, "gx", "gy", "af"),
            P(None, None, "gx", "gy", "af"),
            P("gx", "gy", "af", None, None, None),
            P(None, ("gx", "gy", "af")),
        ),
        check_vma=False,
    )
```

time: 1220 us -> 89.1 us (0.07); the launches traced: 1200 us -> 88.9 us
  waiting for transfers between devices: 756 us -> 0 us
  starting transfers between devices: 133 us -> 0 us
  local copies, waits for them, and re-layouts: 139 us -> 6.66 us
  other arithmetic: 114 us -> 0 us
  Pallas kernels: 0 us -> 81.6 us
  matrix products: 42.7 us -> 0 us
  between operations: 16.1 us -> 0.65 us
    unnamed x2 -> x0, waiting for transfers between devices: 627 us -> none
    ppermute x48 -> x0, starting transfers between devices: 123 us -> none  [the longest x24 63.8 us: extended(): lax.ppermute(lax.slice_in_dim(block, 0, width, axis=dim), axis, backward)]
    pallas_call x0 -> x1, Pallas kernels: none -> 81.6 us  [on_device(): pl.pallas_call(kernel, out_shape=(jax.ShapeDtypeStruct(fields.shape, F32)...]
    slice x29 -> x0, local copies, waits for them, and re-layouts: 71.7 us -> none  [the longest x17 47.1 us: extended(): lax.slice_in_dim(block, block.shape[dim] - width, None, axis=dim)]
    concatenate x17 -> x0, other arithmetic: 70.5 us -> none  [the longest x16 69.3 us: extended(): block = jnp.concatenate([low, block, high], axis=dim)]
    ppermute x48 -> x0, waiting for transfers between devices: 67 us -> none  [the longest x24 55.6 us: extended(): lax.ppermute(lax.slice_in_dim(block, 0, width, axis=dim), axis, backward)]
    all_to_all x1 -> x0, waiting for transfers between devices: 62 us -> none  [on_device(): lax.all_to_all(outgoing, 'gx', split_axis=0, concat_axis=0, tiled=True)]
    ppermute x16 -> x0, local copies, waits for them, and re-layouts: 48.1 us -> none  [the longest x8 24.8 us: extended(): lax.ppermute(lax.slice_in_dim(block, 0, width, axis=dim), axis, backward)]
  transfers between devices with their start and end apart: 50 -> 0, of which waited for: 29 -> 0; matrix products, arithmetic and copies ran while one was open for 4% -> 0% of each run, Pallas kernels for 0% -> 0%
where the time goes in v1:
time: 89.1 us; the launch traced here: 88.9 us
  Pallas kernels  81.6 us (92%)
  local copies, waits for them, and re-layouts  6.66 us (7%)
    pallas_call x1, Pallas kernels, on_device(): pl.pallas_call(kernel, out_shape=(jax.ShapeDtypeStruct(fields.shape, F32)...  81.6 us
    unnamed x10, local copies, waits for them, and re-layouts  5.3 us

profile of v1, /device:TPU:1, one launch (start us, length us, event | category | flops | bytes accessed | tf_op | source)
XLA Modules:
  0.0 88.9 jit_solution(3334679001325156052)
XLA Ops:
  0.6 1.4 %copy.16.owner_ref = s32[64,1]{1,0:T(8,128)} copy(s32[64,1]{0,1:T(1,128)} %bitcast.1) | data formatting | bytes 512 | tf_op jit(solution)/shard_map/reshape | solution.py:455
  2.0 81.6 %fdtd.1 = (f32[6,32,16,128]{3,2,1,0:T(8,128)}, f32[2,3,32,16,128]{4,3,2,1,0:T(8,128)}, f32[1,1,1,8,64,128]{5,4,3,2,1,0:T(8,128)}, f32[8,32]{1,0:T(8,128)}) custom-call(f32[4]{0:T(128)} %eps_ref.1, f32[4]{0:T(128)} %strength_ref.1, f32[4]{0:T(128)} %freq_ref.1, f32[4]{0:T(128)} %damp_ref.1, f32[8,64]{1,0:T(8,128)} %constant.8.clone.weight_ref, ...), custom_call_target="tpu_custom_call" | custom-call | tf_op jit(solution)/shard_map/fdtd/pallas_call | solution.py:424
  83.6 0.0 copy-start
  83.6 2.9 %copy.21 = f32[6,32,16,128]{3,2,1,0:T(8,128)} copy(f32[6,32,16,128]{3,2,1,0:T(8,128)} %get-tuple-element.8) | data formatting | bytes 3145728
  86.5 0.0 copy-done
  86.5 0.0 copy-start.1
  86.5 0.0 copy-start.2
  86.5 1.1 %copy.22 = f32[2,3,32,16,128]{4,3,2,1,0:T(8,128)} copy(f32[2,3,32,16,128]{4,3,2,1,0:T(8,128)S(1)} %copy-done) | data formatting | bytes 3145728
  87.6 0.0 copy-done.1
  87.6 0.7 copy.23
  88.3 0.0 copy-done.2
  88.3 0.6 copy.24
Async XLA Ops:
  83.6 2.9 %copy-start = (f32[2,3,32,16,128]{4,3,2,1,0:T(8,128)S(1)}, f32[2,3,32,16,128]{4,3,2,1,0:T(8,128)}, u32[]{:S(2)}) copy-start(f32[2,3,32,16,128]{4,3,2,1,0:T(8,128)} %get-tuple-element.9) | copy-start | bytes 4718596
  86.5 1.1 %copy-start.1 = (f32[1,1,1,8,64,128]{5,4,3,2,1,0:T(8,128)S(1)}, f32[1,1,1,8,64,128]{5,4,3,2,1,0:T(8,128)}, u32[]{:S(2)}) copy-start(f32[1,1,1,8,64,128]{5,4,3,2,1,0:T(8,128)} %get-tuple-element.10) | copy-start | bytes 786436
  86.5 1.9 %copy-start.2 = (f32[8,32]{1,0:T(8,128)S(1)}, f32[8,32]{1,0:T(8,128)}, u32[]{:S(2)}) copy-start(f32[8,32]{1,0:T(8,128)} %get-tuple-element.11) | copy-start | bytes 3076

commit v2 on v1

--- a/solution.py
+++ b/solution.py
@@ -55,12 +55,13 @@
     eps_ref, strength_ref, freq_ref, damp_ref, weight_ref, owner_ref,
     fields_ref, pol_ref, mat_ref, spread_hbm, ztab_hbm, ytab_hbm,
     out_f, out_p, out_s, out_far,
-    E, H, PQ, mat, coef, stage, samp, ztab, ytab, spread, part, parts,
+    E0, E1, H, P0, P1, mat, coef, stage, samp, ztab, ytab, spread, part, parts,
     local_sem, swap_send, swap_recv, halo_send, halo_recv, first_send, first_recv,
     samp_send, samp_recv, far_send, far_recv, out_sem, out_send, out_recv,
 ):
     gx, gy, c = lax.axis_index("gx"), lax.axis_index("gy"), lax.axis_index("af")
     place = 2 * gx + c
+    E = (E0, E1)
     other = 1 - c
     has_up, has_down = place < 2 * NGX - 1, place > 0
     has_right, has_left = gy < NGY - 1, gy > 0
@@ -99,9 +100,10 @@
     here = pl.ds(c * HX, HX)
     there = pl.ds(other * HX, HX)
     loads = [
-        (fields_ref.at[0:3, here], E.at[0, :, c, 1:HX + 1, 8:24]),
+        (fields_ref.at[0:3, here], E0.at[:, c, 1:HX + 1, 8:24]),
         (fields_ref.at[3:6, here], H.at[:, c, 1:HX + 1, 8:24]),
-        (pol_ref.at[:, :, here], PQ.at[:, :, c]),
+        (pol_ref.at[0, :, here], P0.at[:, c]),
+        (pol_ref.at[1, :, here], P1.at[:, c]),
         (mat_ref.at[here], mat.at[c]),
         (ztab_hbm.at[gx], ztab),
         (ytab_hbm.at[me, gx], ytab),
@@ -116,7 +118,7 @@
         for p in range(2):
             for d in (1, 2):
                 for z in range(2):
-                    E[p, d, z, HX + 1, 0:24] = jnp.zeros((24, 128), F32)
+                    E[p][d, z, HX + 1, 0:24] = jnp.zeros((24, 128), F32)
 
     @pl.when(jnp.logical_not(has_right))
     def _():
@@ -125,7 +127,7 @@
             for p in range(2):
                 for d in (0, 2):
                     for z in range(2):
-                        E[p, d, z, i, 24:32] = jnp.zeros((8, 128), F32)
+                        E[p][d, z, i, 24:32] = jnp.zeros((8, 128), F32)
 
     count = (
         NGY * NAF - 1
@@ -136,9 +138,10 @@
     pl.semaphore_wait(barrier, count)
 
     swaps = [
-        (fields_ref.at[0:3, there], E.at[0, :, c, 1:HX + 1, 8:24]),
+        (fields_ref.at[0:3, there], E0.at[:, c, 1:HX + 1, 8:24]),
         (fields_ref.at[3:6, there], H.at[:, c, 1:HX + 1, 8:24]),
-        (pol_ref.at[:, :, there], PQ.at[:, :, c]),
+        (pol_ref.at[0, :, there], P0.at[:, c]),
+        (pol_ref.at[1, :, there], P1.at[:, c]),
         (mat_ref.at[there], mat.at[c]),
     ]
     swaps = [
@@ -161,20 +164,21 @@
                 device_id=device, device_id_type=MESH,
             )
 
+        e = E[p]
         own, rows = pl.ds(1, HX), pl.ds(8, BY)
         return [
-            (has_up, has_down, message(0, E.at[p, :, :, HX, rows], E.at[p, :, :, 0, rows], up)),
-            (has_down, has_up, message(1, E.at[p, 1:3, :, 1, rows], E.at[p, 1:3, :, HX + 1, rows], down)),
-            (has_right, has_left, message(2, E.at[p, :, :, own, 23:24], E.at[p, :, :, own, 7:8], right)),
-            (has_left, has_right, message(3, E.at[p, 0, :, own, 8:9], E.at[p, 0, :, own, 24:25], left)),
-            (has_left, has_right, message(4, E.at[p, 2, :, own, 8:9], E.at[p, 2, :, own, 24:25], left)),
+            (has_up, has_down, message(0, e.at[:, :, HX, rows], e.at[:, :, 0, rows], up)),
+            (has_down, has_up, message(1, e.at[1:3, :, 1, rows], e.at[1:3, :, HX + 1, rows], down)),
+            (has_right, has_left, message(2, e.at[:, :, own, 23:24], e.at[:, :, own, 7:8], right)),
+            (has_left, has_right, message(3, e.at[0, :, own, 8:9], e.at[0, :, own, 24:25], left)),
+            (has_left, has_right, message(4, e.at[2, :, own, 8:9], e.at[2, :, own, 24:25], left)),
             (
                 jnp.logical_and(has_up, has_left), jnp.logical_and(has_down, has_right),
-                message(5, E.at[p, 0, :, HX, 8:9], E.at[p, 0, :, 0, 24:25], up_left),
+                message(5, e.at[0, :, HX, 8:9], e.at[0, :, 0, 24:25], up_left),
             ),
             (
                 jnp.logical_and(has_down, has_right), jnp.logical_and(has_up, has_left),
-                message(6, E.at[p, 1, :, 1, 23:24], E.at[p, 1, :, HX + 1, 7:8], down_right),
+                message(6, e.at[1, :, 1, 23:24], e.at[1, :, HX + 1, 7:8], down_right),
             ),
         ]
 
@@ -208,10 +212,10 @@
     ]
     start(h_layers)
     start(halos(0))
-    for i in range(2, 4):
+    for i in range(2, 5):
         loads[i].wait()
         swaps[i].wait()
-    for copy in loads[4:]:
+    for copy in loads[5:]:
         copy.wait()
 
     rates = [[], [], [], []]
@@ -247,23 +251,21 @@
         r0, r1 = (pltpu.roll(x, 1, 1) for x in v)
         return jnp.where(first_lane, 0.0, r0), jnp.where(first_lane, r0, r1)
 
-    def magnetic(p, i, j, keep):
+    def magnetic(e, i, j, keep=None):
         r = pl.ds(8 * j, 8)
         r1 = pl.ds(8 * j + 1, 8)
-        ex, ey, ez = ([E[p, d, z, i, r] for z in range(2)] for d in range(3))
+        ex, ey, ez = ([e[d, z, i, r] for z in range(2)] for d in range(3))
         ex_z, ey_z = ahead_z(ex), ahead_z(ey)
         for z in range(2):
-            hx = H[0, z, i, r] - DT * ((E[p, 2, z, i, r1] - ez[z]) - (ey_z[z] - ey[z]))
-            hy = H[1, z, i, r] - DT * ((ex_z[z] - ex[z]) - (E[p, 2, z, i + 1, r] - ez[z]))
-            hz = H[2, z, i, r] - DT * ((E[p, 1, z, i + 1, r] - ey[z]) - (E[p, 0, z, i, r1] - ex[z]))
-            if keep is not None:
-                hx, hy, hz = (jnp.where(keep, h, 0.0) for h in (hx, hy, hz))
-            H[0, z, i, r] = hx
-            H[1, z, i, r] = hy
-            H[2, z, i, r] = hz
-
-    def electric(p, i, j):
-        q = 1 - p
+            hx = H[0, z, i, r] - DT * ((e[2, z, i, r1] - ez[z]) - (ey_z[z] - ey[z]))
+            hz = H[2, z, i, r] - DT * ((e[1, z, i + 1, r] - ey[z]) - (e[0, z, i, r1] - ex[z]))
+            H[0, z, i, r] = hx if keep is None else jnp.where(keep, hx, 0.0)
+            H[2, z, i, r] = hz if keep is None else jnp.where(keep, hz, 0.0)
+            if j > 0:
+                hy = H[1, z, i, r] - DT * ((ex_z[z] - ex[z]) - (e[2, z, i + 1, r] - ez[z]))
+                H[1, z, i, r] = hy if keep is None else jnp.where(keep, hy, 0.0)
+
+    def electric(e, e_new, now_ref, old_ref, i, j):
         r = pl.ds(8 * j, 8)
         r1 = pl.ds(8 * j - 1, 8)
         s = pl.ds(8 * (j - 1), 8)
@@ -277,11 +279,11 @@
             )
             keep, back, drive, inverse = (coef[k, z, i - 1, s] for k in range(4))
             for d in range(3):
-                e = E[p, d, z, i, r]
-                now = PQ[p, d, z, i - 1, s]
-                new = keep * now + back * PQ[q, d, z, i - 1, s] + drive * e
-                PQ[q, d, z, i - 1, s] = new
-                E[q, d, z, i, r] = e + inverse * (DT * curl[d] - (new - now))
+                value = e[d, z, i, r]
+                now = now_ref[d, z, i - 1, s]
+                new = keep * now + back * old_ref[d, z, i - 1, s] + drive * value
+                old_ref[d, z, i - 1, s] = new
+                e_new[d, z, i, r] = value + inverse * (DT * curl[d] - (new - now))
 
     def sample_copy(n, g, t):
         return pltpu.make_async_remote_copy(
@@ -298,28 +300,38 @@
             def _():
                 act(g, 1)
 
-    @pl.loop(0, STEPS)
-    def _(n):
-        p = lax.rem(n, 2)
-
-        @pl.when(n > 0)
+    def start_next(n, p):
+        @pl.when(n < STEPS - 1)
         def _():
             start(halos(p))
 
+    def step(n, p):
+        e, e_new = E[p], E[1 - p]
+        now_ref, old_ref = (P0, P1) if p == 0 else (P1, P0)
+
+        @pl.loop(0, 3)
+        def _(b):
+            for u in range(5):
+                magnetic(e, 1 + 5 * b + u, 1)
+
         finish(halos(p))
-        magnetic(p, 0, 1, has_down)
-        magnetic(p, 0, 2, has_down)
-
-        @pl.loop(1, HX + 1)
-        def _(i):
-            magnetic(p, i, 0, has_left)
-            magnetic(p, i, 1, None)
-            magnetic(p, i, 2, None)
-
-        @pl.loop(1, HX + 1)
-        def _(i):
-            electric(p, i, 1)
-            electric(p, i, 2)
+        magnetic(e, 0, 1, has_down)
+        magnetic(e, 0, 2, has_down)
+        magnetic(e, HX, 1)
+
+        @pl.loop(0, 2)
+        def _(b):
+            for u in range(8):
+                magnetic(e, 1 + 8 * b + u, 0, has_left)
+                magnetic(e, 1 + 8 * b + u, 2)
+
+        @pl.loop(0, 4)
+        def _(b):
+            for u in range(4):
+                electric(e, e_new, now_ref, old_ref, 1 + 4 * b + u, 1)
+                electric(e, e_new, now_ref, old_ref, 1 + 4 * b + u, 2)
+
+        start_next(n, 1 - p)
 
         @pl.when(is_holder)
         def _():
@@ -329,16 +341,22 @@
 
             for t in range(2):
                 for d in range(2):
-                    stage[n, t, d] = E[1 - p, d + 1, t, 1, 8:24]
+                    stage[n, t, d] = e_new[d + 1, t, 1, 8:24]
                     stage[n, t, d + 2] = H[d + 1, t, 1, 8:24]
             each_receiver(lambda g, t: sample_copy(n, g, t).start())
             samp[n] = stage[n, 1]
 
-    e_out = lambda z: (E.at[0, :, z, own, rows], out_f.at[0:3, here])
+    @pl.loop(0, STEPS // 2)
+    def _(b):
+        step(2 * b, 0)
+        step(2 * b + 1, 1)
+
+    e_out = lambda z: (E0.at[:, z, own, rows], out_f.at[0:3, here])
     h_out = lambda z: (H.at[:, z, own, rows], out_f.at[3:6, here])
-    p_out = lambda z: (PQ.at[:, :, z], out_p.at[:, :, here])
+    p_out = lambda z: (P0.at[:, z], out_p.at[0, :, here])
+    q_out = lambda z: (P1.at[:, z], out_p.at[1, :, here])
     sends = []
-    for k, out in enumerate((e_out, h_out, p_out)):
+    for k, out in enumerate((e_out, h_out, p_out, q_out)):
         s, d = out(other)
         sends.append(pltpu.make_async_remote_copy(
             src_ref=s, dst_ref=d, send_sem=out_send.at[k], recv_sem=out_recv.at[k],
@@ -390,12 +408,13 @@
     mine = (owner_ref[...] == gx).astype(F32)
     row = lax.broadcasted_iota(jnp.int32, (64, 64), 0)
     col = lax.broadcasted_iota(jnp.int32, (64, 64), 1)
-    rank = jnp.dot((col < row).astype(F32), mine, precision=HIGHEST, preferred_element_type=F32)
-    slot = lax.broadcasted_iota(jnp.int32, (64, 128), 1).astype(F32)
+    rank = jnp.dot(
+        jnp.broadcast_to(mine, (8, 64)), (row < col).astype(F32), precision=HIGHEST, preferred_element_type=F32
+    )
+    slot = lax.broadcasted_iota(jnp.int32, (8, 64), 0).astype(F32)
     picked = jnp.where(rank == slot, mine, 0.0)
     chosen = [
-        lax.dot_general(picked, rows_of[n], (((0,), (0,)), ((), ())), precision=HIGHEST, preferred_element_type=F32)
-        for n in range(STEPS)
+        jnp.dot(picked, rows_of[n], precision=HIGHEST, preferred_element_type=F32) for n in range(STEPS)
     ]
     for s in range(SLOTS):
         for k in range(2 * NF // 8):
@@ -424,17 +443,19 @@
     return pl.pallas_call(
         kernel,
         out_shape=(
-            jax.ShapeDtypeStruct(fields.shape, F32),
-            jax.ShapeDtypeStruct(polarization.shape, F32),
-            jax.ShapeDtypeStruct((1, 1, 1, SLOTS, 2 * NF, BZ), F32),
-            jax.ShapeDtypeStruct((8, 32), F32),
+            pltpu.VMEM(fields.shape, F32),
+            pltpu.VMEM(polarization.shape, F32),
+            pltpu.VMEM((1, 1, 1, SLOTS, 2 * NF, BZ), F32),
+            pltpu.VMEM((8, 32), F32),
         ),
         in_specs=[smem] * 5 + [vmem] + [hbm] * 6,
-        out_specs=(hbm, hbm, vmem, vmem),
+        out_specs=(vmem, vmem, vmem, vmem),
         scratch_shapes=[
-            pltpu.VMEM((2, 3, 2, HX + 2, 32, 128), F32),
+            pltpu.VMEM((3, 2, HX + 2, 32, 128), F32),
+            pltpu.VMEM((3, 2, HX + 2, 32, 128), F32),
             pltpu.VMEM((3, 2, HX + 1, 24, 128), F32),
-            pltpu.VMEM((2, 3, 2, HX, BY, 128), F32),
+            pltpu.VMEM((3, 2, HX, BY, 128), F32),
+            pltpu.VMEM((3, 2, HX, BY, 128), F32),
             pltpu.VMEM((2, HX, BY, 128), jnp.int32),
             pltpu.VMEM((4, 2, HX, BY, 128), F32),
             pltpu.VMEM((STEPS, 2, 4, BY, 128), F32),
@@ -444,15 +465,15 @@
             pltpu.VMEM((STEPS, 2 * NF, 128), F32),
             pltpu.VMEM((2, 8, 128), F32),
             pltpu.VMEM((8, 8, 128), F32),
-            dma(7), dma(4), dma(4), dma(7), dma(2, 7), dma(3), dma(3),
-            dma(NGX, 2), dma(STEPS), dma(8), dma(8), dma(3), dma(3), dma(3),
+            dma(8), dma(5), dma(5), dma(7), dma(2, 7), dma(3), dma(3),
+            dma(NGX, 2), dma(STEPS), dma(8), dma(8), dma(4), dma(4), dma(4),
         ],
         compiler_params=pltpu.CompilerParams(
             collective_id=0, has_side_effects=True, vmem_limit_bytes=56 << 20
         ),
         name="fdtd",
     )(
-        eps_inf, pole_strength, pole_freq, damping, weights, owner.reshape(64, 1),
+        eps_inf, pole_strength, pole_freq, damping, weights, owner.reshape(1, 64),
         fields, polarization, material, spread, z_table, y_table,
     )
 

time: 89.1 us -> 73.7 us (0.83)
  Pallas kernels: 81.6 us -> 69.3 us
  local copies, waits for them, and re-layouts: 6.66 us -> 3.58 us
    pallas_call x1, Pallas kernels: 81.6 us -> 69.3 us  [on_device(): pl.pallas_call(kernel, out_shape=(pltpu.VMEM(fields.shape, F32), pltpu.VM...]
    unnamed x10 -> x4, local copies, waits for them, and re-layouts: 5.3 us -> 3.58 us
    reshape x1 -> x0, local copies, waits for them, and re-layouts: 1.36 us -> none  [on_device(): owner.reshape(64, 1)]
where the time goes in v2:
time: 73.7 us; the launch traced here: 73.6 us
  Pallas kernels  69.3 us (94%)
  local copies, waits for them, and re-layouts  3.58 us (5%)
    pallas_call x1, Pallas kernels, on_device(): pl.pallas_call(kernel, out_shape=(pltpu.VMEM(fields.shape, F32), pltpu.VM...  69.3 us
    unnamed x4, local copies, waits for them, and re-layouts  3.58 us

profile of v2, /device:TPU:1, one launch (start us, length us, event | category | flops | bytes accessed | tf_op | source)
XLA Modules:
  0.0 73.6 jit_solution(5860403430326837667)
XLA Ops:
  0.6 69.3 %fdtd.1 = (f32[6,32,16,128]{3,2,1,0:T(8,128)S(1)}, f32[2,3,32,16,128]{4,3,2,1,0:T(8,128)S(1)}, f32[1,1,1,8,64,128]{5,4,3,2,1,0:T(8,128)S(1)}, f32[8,32]{1,0:T(8,128)S(1)}) custom-call(f32[4]{0:T(128)} %eps_ref.1, f32[4]{0:T(128)} %strength_ref.1, f32[4]{0:T(128)} %freq_ref.1, f32[4]{0:T(128)} %damp_ref.1, f32[8,64]{1,0:T(8,128)} %constant.8.clone.weight_ref, ...), custom_call_target="tpu_custom_call" | custom-call | tf_op jit(solution)/shard_map/fdtd/pallas_call | solution.py:443
  70.0 1.1 %copy.20 = f32[6,32,16,128]{3,2,1,0:T(8,128)} copy(f32[6,32,16,128]{3,2,1,0:T(8,128)S(1)} %get-tuple-element.4) | data formatting | bytes 3145728
  71.1 0.6 copy.23
  71.7 0.7 copy.22
  72.4 1.1 %copy.21 = f32[2,3,32,16,128]{4,3,2,1,0:T(8,128)} copy(f32[2,3,32,16,128]{4,3,2,1,0:T(8,128)S(1)} %get-tuple-element.5) | data formatting | bytes 3145728

commit v3 on v2

--- a/solution.py
+++ b/solution.py
@@ -16,6 +16,7 @@
 NGX, NGY, NAF = 16, 4, 2
 BX, BY, BZ = 32, 16, 128
 HX = BX // 2
+ROW = 4
 SLOTS = 8
 DT = 0.5
 MESH = pl.DeviceIdType.MESH
@@ -72,6 +73,11 @@
     down_right = (gx - other, gy + 1, other)
     partner = (gx, gy, other)
     is_holder = jnp.logical_and(gx == NGX - 1, c == 1)
+    row_end = gx // ROW * ROW + ROW - 1
+    is_last_row = gx // ROW == NGX // ROW - 1
+    is_relay = jnp.logical_and(gx == row_end, jnp.logical_not(is_last_row))
+    fed_by_relay = jnp.logical_and(gx != row_end, jnp.logical_not(is_last_row))
+    fed_by_holder = jnp.logical_or(is_relay, jnp.logical_and(is_last_row, gx != row_end))
     me = gy * NAF + c
 
     barrier = pltpu.get_barrier_semaphore()
@@ -93,7 +99,11 @@
         def _(device=device):
             greet(device)
 
-    @pl.when(jnp.logical_not(is_holder))
+    @pl.when(fed_by_relay)
+    def _():
+        greet((row_end, gy, c))
+
+    @pl.when(fed_by_holder)
     def _():
         greet((NGX - 1, gy, 1))
 
@@ -133,7 +143,8 @@
         NGY * NAF - 1
         + across_up.astype(jnp.int32) + across_down.astype(jnp.int32)
         + across_up_left.astype(jnp.int32) + across_down_right.astype(jnp.int32)
-        + jnp.where(is_holder, 2 * NGX - 1, 0)
+        + jnp.where(is_holder, 2 * (NGX // ROW + ROW - 2), 0)
+        + jnp.where(is_relay, ROW - 1, 0)
     )
     pl.semaphore_wait(barrier, count)
 
@@ -285,20 +296,34 @@
                 old_ref[d, z, i - 1, s] = new
                 e_new[d, z, i, r] = value + inverse * (DT * curl[d] - (new - now))
 
-    def sample_copy(n, g, t):
+    def sample_copy(n, k, device):
+        g, t = device
         return pltpu.make_async_remote_copy(
-            src_ref=stage.at[n, t], dst_ref=samp.at[n], send_sem=samp_send.at[g, t], recv_sem=samp_recv.at[n],
+            src_ref=stage.at[n, t], dst_ref=samp.at[n], send_sem=samp_send.at[k], recv_sem=samp_recv.at[n],
             device_id=(g, gy, t), device_id_type=MESH,
         )
 
-    def each_receiver(act):
-        @pl.loop(0, NGX)
-        def _(g):
-            act(g, 0)
-
-            @pl.when(g < NGX - 1)
+    receivers = [(NGX - 1, 0)]
+    receivers += [(ROW * k + ROW - 1, t) for k in range(NGX // ROW - 1) for t in range(2)]
+    receivers += [(NGX - ROW + k, t) for k in range(ROW - 1) for t in range(2)]
+
+    def relay_copy(n, k):
+        return pltpu.make_async_remote_copy(
+            src_ref=samp.at[n], dst_ref=samp.at[n], send_sem=samp_send.at[k], recv_sem=samp_recv.at[n],
+            device_id=(row_end - 1 - k, gy, c), device_id_type=MESH,
+        )
+
+    def relay(n):
+        @pl.when(is_relay)
+        def _():
+            @pl.when(n > 0)
             def _():
-                act(g, 1)
+                for k in range(ROW - 1):
+                    relay_copy(n - 1, k).wait_send()
+
+            relay_copy(n, 0).wait_recv()
+            for k in range(ROW - 1):
+                relay_copy(n, k).start()
 
     def start_next(n, p):
         @pl.when(n < STEPS - 1)
@@ -333,17 +358,23 @@
 
         start_next(n, 1 - p)
 
+        @pl.when(n > 0)
+        def _():
+            relay(n - 1)
+
         @pl.when(is_holder)
         def _():
             @pl.when(n > 0)
             def _():
-                each_receiver(lambda g, t: sample_copy(n - 1, g, t).wait_send())
+                for k, device in enumerate(receivers):
+                    sample_copy(n - 1, k, device).wait_send()
 
             for t in range(2):
                 for d in range(2):
                     stage[n, t, d] = e_new[d + 1, t, 1, 8:24]
                     stage[n, t, d + 2] = H[d + 1, t, 1, 8:24]
-            each_receiver(lambda g, t: sample_copy(n, g, t).start())
+            for k, device in enumerate(receivers):
+                sample_copy(n, k, device).start()
             samp[n] = stage[n, 1]
 
     @pl.loop(0, STEPS // 2)
@@ -367,14 +398,17 @@
     for copy in sends:
         copy.start()
 
+    relay(STEPS - 1)
+
     @pl.when(is_holder)
     def _():
-        each_receiver(lambda g, t: sample_copy(STEPS - 1, g, t).wait_send())
-
-    @pl.when(jnp.logical_not(is_holder))
+        for k, device in enumerate(receivers):
+            sample_copy(STEPS - 1, k, device).wait_send()
+
+    @pl.when(jnp.logical_not(jnp.logical_or(is_holder, is_relay)))
     def _():
         for n in range(STEPS):
-            sample_copy(n, 0, 0).wait_recv()
+            sample_copy(n, 0, (0, 0)).wait_recv()
 
     rows_of = [samp[n].reshape(4 * BY, 128) for n in range(STEPS)]
     for f in range(2):
@@ -432,6 +466,11 @@
     out_far[...] = total[:, :32]
     for copy in sends:
         copy.wait()
+
+    @pl.when(is_relay)
+    def _():
+        for k in range(ROW - 1):
+            relay_copy(STEPS - 1, k).wait_send()
 
 
 def on_device(constants, fields, polarization, material, eps_inf, pole_strength, pole_freq, damping, owner):
@@ -466,7 +505,7 @@
             pltpu.VMEM((2, 8, 128), F32),
             pltpu.VMEM((8, 8, 128), F32),
             dma(8), dma(5), dma(5), dma(7), dma(2, 7), dma(3), dma(3),
-            dma(NGX, 2), dma(STEPS), dma(8), dma(8), dma(4), dma(4), dma(4),
+            dma(13), dma(STEPS), dma(8), dma(8), dma(4), dma(4), dma(4),
         ],
         compiler_params=pltpu.CompilerParams(
             collective_id=0, has_side_effects=True, vmem_limit_bytes=56 << 20

time: 73.7 us -> 62 us (0.84)
  Pallas kernels: 69.3 us -> 57.7 us
    pallas_call x1, Pallas kernels: 69.3 us -> 57.7 us  [on_device(): pl.pallas_call(kernel, out_shape=(pltpu.VMEM(fields.shape, F32), pltpu.VM...]
where the time goes in v3:
time: 62 us; the launch traced here: 61.9 us
  Pallas kernels  57.7 us (93%)
  local copies, waits for them, and re-layouts  3.58 us (6%)
  between operations  0.64 us (1%)
    pallas_call x1, Pallas kernels, on_device(): pl.pallas_call(kernel, out_shape=(pltpu.VMEM(fields.shape, F32), pltpu.VM...  57.7 us
    unnamed x4, local copies, waits for them, and re-layouts  3.58 us

profile of v3, /device:TPU:1, one launch (start us, length us, event | category | flops | bytes accessed | tf_op | source)
XLA Modules:
  0.0 61.9 jit_solution(17973878619507739926)
XLA Ops:
  0.6 57.7 %fdtd.1 = (f32[6,32,16,128]{3,2,1,0:T(8,128)S(1)}, f32[2,3,32,16,128]{4,3,2,1,0:T(8,128)S(1)}, f32[1,1,1,8,64,128]{5,4,3,2,1,0:T(8,128)S(1)}, f32[8,32]{1,0:T(8,128)S(1)}) custom-call(f32[4]{0:T(128)} %eps_ref.1, f32[4]{0:T(128)} %strength_ref.1, f32[4]{0:T(128)} %freq_ref.1, f32[4]{0:T(128)} %damp_ref.1, f32[8,64]{1,0:T(8,128)} %constant.8.clone.weight_ref, ...), custom_call_target="tpu_custom_call" | custom-call | tf_op jit(solution)/shard_map/fdtd/pallas_call | solution.py:482
  58.3 1.1 %copy.20 = f32[6,32,16,128]{3,2,1,0:T(8,128)} copy(f32[6,32,16,128]{3,2,1,0:T(8,128)S(1)} %get-tuple-element.4) | data formatting | bytes 3145728
  59.4 0.6 copy.23
  60.0 0.7 %copy.22 = f32[1,1,1,8,64,128]{5,4,3,2,1,0:T(8,128)} copy(f32[1,1,1,8,64,128]{5,4,3,2,1,0:T(8,128)S(1)} %get-tuple-element.6) | data formatting | bytes 524288
  60.7 1.1 %copy.21 = f32[2,3,32,16,128]{4,3,2,1,0:T(8,128)} copy(f32[2,3,32,16,128]{4,3,2,1,0:T(8,128)S(1)} %get-tuple-element.5) | data formatting | bytes 3145728

commit v4 on v3

--- a/solution.py
+++ b/solution.py
@@ -56,7 +56,7 @@
     eps_ref, strength_ref, freq_ref, damp_ref, weight_ref, owner_ref,
     fields_ref, pol_ref, mat_ref, spread_hbm, ztab_hbm, ytab_hbm,
     out_f, out_p, out_s, out_far,
-    E0, E1, H, P0, P1, mat, coef, stage, samp, ztab, ytab, spread, part, parts,
+    E0, E1, H, P0, P1, mat, coef, stage, samp, ztab, ytab, spread, sums, part, parts,
     local_sem, swap_send, swap_recv, halo_send, halo_recv, first_send, first_recv,
     samp_send, samp_recv, far_send, far_recv, out_sem, out_send, out_recv,
 ):
@@ -164,9 +164,6 @@
     ]
     for copy in swaps:
         copy.start()
-    for i in range(2):
-        loads[i].wait()
-        swaps[i].wait()
 
     def halos(p):
         def message(k, src, dst, device):
@@ -177,12 +174,9 @@
 
         e = E[p]
         own, rows = pl.ds(1, HX), pl.ds(8, BY)
-        return [
+        along_x = [
             (has_up, has_down, message(0, e.at[:, :, HX, rows], e.at[:, :, 0, rows], up)),
             (has_down, has_up, message(1, e.at[1:3, :, 1, rows], e.at[1:3, :, HX + 1, rows], down)),
-            (has_right, has_left, message(2, e.at[:, :, own, 23:24], e.at[:, :, own, 7:8], right)),
-            (has_left, has_right, message(3, e.at[0, :, own, 8:9], e.at[0, :, own, 24:25], left)),
-            (has_left, has_right, message(4, e.at[2, :, own, 8:9], e.at[2, :, own, 24:25], left)),
             (
                 jnp.logical_and(has_up, has_left), jnp.logical_and(has_down, has_right),
                 message(5, e.at[0, :, HX, 8:9], e.at[0, :, 0, 24:25], up_left),
@@ -192,6 +186,12 @@
                 message(6, e.at[1, :, 1, 23:24], e.at[1, :, HX + 1, 7:8], down_right),
             ),
         ]
+        along_y = [
+            (has_right, has_left, message(2, e.at[:, :, own, 23:24], e.at[:, :, own, 7:8], right)),
+            (has_left, has_right, message(3, e.at[0, :, own, 8:9], e.at[0, :, own, 24:25], left)),
+            (has_left, has_right, message(4, e.at[2, :, own, 8:9], e.at[2, :, own, 24:25], left)),
+        ]
+        return along_y, along_x
 
     def start(messages):
         for receiver, _, copy in messages:
@@ -221,8 +221,14 @@
         (has_right, has_left, first(1, H.at[0, :, own, 23:24], H.at[0, :, own, 7:8], right)),
         (has_right, has_left, first(2, H.at[2, :, own, 23:24], H.at[2, :, own, 7:8], right)),
     ]
+    along_y, along_x = halos(0)
+    loads[0].wait()
+    swaps[0].wait()
+    start(along_x)
+    start(along_y)
+    loads[1].wait()
+    swaps[1].wait()
     start(h_layers)
-    start(halos(0))
     for i in range(2, 5):
         loads[i].wait()
         swaps[i].wait()
@@ -328,33 +334,44 @@
     def start_next(n, p):
         @pl.when(n < STEPS - 1)
         def _():
-            start(halos(p))
+            along_y, along_x = halos(p)
+            start(along_x)
+            start(along_y)
 
     def step(n, p):
         e, e_new = E[p], E[1 - p]
         now_ref, old_ref = (P0, P1) if p == 0 else (P1, P0)
+
+        along_y, along_x = halos(p)
 
         @pl.loop(0, 3)
         def _(b):
             for u in range(5):
                 magnetic(e, 1 + 5 * b + u, 1)
 
-        finish(halos(p))
+        finish(along_y)
+
+        @pl.loop(0, 3)
+        def _(b):
+            for u in range(5):
+                magnetic(e, 1 + 5 * b + u, 0, has_left)
+                magnetic(e, 1 + 5 * b + u, 2)
+
+        @pl.loop(0, 2)
+        def _(b):
+            for u in range(7):
+                electric(e, e_new, now_ref, old_ref, 2 + 7 * b + u, 1)
+                electric(e, e_new, now_ref, old_ref, 2 + 7 * b + u, 2)
+
+        finish(along_x)
         magnetic(e, 0, 1, has_down)
         magnetic(e, 0, 2, has_down)
-        magnetic(e, HX, 1)
-
-        @pl.loop(0, 2)
-        def _(b):
-            for u in range(8):
-                magnetic(e, 1 + 8 * b + u, 0, has_left)
-                magnetic(e, 1 + 8 * b + u, 2)
-
-        @pl.loop(0, 4)
-        def _(b):
-            for u in range(4):
-                electric(e, e_new, now_ref, old_ref, 1 + 4 * b + u, 1)
-                electric(e, e_new, now_ref, old_ref, 1 + 4 * b + u, 2)
+        magnetic(e, HX, 0, has_left)
+        for j in (1, 2):
+            magnetic(e, HX, j)
+        for i in (1, HX):
+            for j in (1, 2):
+                electric(e, e_new, now_ref, old_ref, i, j)
 
         start_next(n, 1 - p)
 
@@ -398,27 +415,57 @@
     for copy in sends:
         copy.start()
 
-    relay(STEPS - 1)
-
-    @pl.when(is_holder)
-    def _():
-        for k, device in enumerate(receivers):
-            sample_copy(STEPS - 1, k, device).wait_send()
-
-    @pl.when(jnp.logical_not(jnp.logical_or(is_holder, is_relay)))
-    def _():
-        for n in range(STEPS):
+    last = STEPS - 1
+    is_end = jnp.logical_not(jnp.logical_or(is_holder, is_relay))
+
+    @pl.when(is_end)
+    def _():
+        for n in range(last):
             sample_copy(n, 0, (0, 0)).wait_recv()
 
-    rows_of = [samp[n].reshape(4 * BY, 128) for n in range(STEPS)]
+    def sample(n):
+        return samp[n].reshape(4 * BY, 128)
+
+    def weight(n, f):
+        return weight_ref[n, 2 * gx + f], weight_ref[n, NF + 2 * gx + f]
+
     for f in range(2):
-        real = weight_ref[0, 2 * gx + f] * rows_of[0]
-        imag = weight_ref[0, NF + 2 * gx + f] * rows_of[0]
-        for n in range(1, STEPS):
-            real += weight_ref[n, 2 * gx + f] * rows_of[n]
-            imag += weight_ref[n, NF + 2 * gx + f] * rows_of[n]
-        both = jnp.concatenate([real, imag], axis=0)
-        inner = jnp.dot(both, ztab[f], precision=HIGHEST, preferred_element_type=F32)
+        for k in range(2):
+            total = weight(0, f)[k] * sample(0)
+            for n in range(1, last):
+                total += weight(n, f)[k] * sample(n)
+            sums[f, 64 * k:64 * k + 64] = total
+
+    mine = (owner_ref[...] == gx).astype(F32)
+    row = lax.broadcasted_iota(jnp.int32, (64, 64), 0)
+    col = lax.broadcasted_iota(jnp.int32, (64, 64), 1)
+    rank = jnp.dot(
+        jnp.broadcast_to(mine, (8, 64)), (row < col).astype(F32), precision=HIGHEST, preferred_element_type=F32
+    )
+    slot = lax.broadcasted_iota(jnp.int32, (8, 64), 0).astype(F32)
+    picked = jnp.where(rank == slot, mine, 0.0)
+
+    def choose(n):
+        return jnp.dot(picked, sample(n), precision=HIGHEST, preferred_element_type=F32)
+
+    chosen = [choose(n) for n in range(last)]
+    for s in range(SLOTS):
+        for k in range(2 * NF // 8):
+            total = spread[0, 8 * k:8 * k + 8] * chosen[0][s:s + 1]
+            for n in range(1, last):
+                total += spread[n, 8 * k:8 * k + 8] * chosen[n][s:s + 1]
+            out_s[0, 0, 0, s, 8 * k:8 * k + 8] = total
+
+    relay(last)
+
+    @pl.when(is_end)
+    def _():
+        sample_copy(last, 0, (0, 0)).wait_recv()
+
+    for f in range(2):
+        for k in range(2):
+            sums[f, 64 * k:64 * k + 64] += weight(last, f)[k] * sample(last)
+        inner = jnp.dot(sums[f], ztab[f], precision=HIGHEST, preferred_element_type=F32)
         inner_real = inner[:64, :128] - inner[64:, 128:]
         inner_imag = inner[:64, 128:] + inner[64:, :128]
         cos_y, sin_y = ytab[f, 0], ytab[f, 1]
@@ -439,23 +486,10 @@
     for copy in far:
         copy.start()
 
-    mine = (owner_ref[...] == gx).astype(F32)
-    row = lax.broadcasted_iota(jnp.int32, (64, 64), 0)
-    col = lax.broadcasted_iota(jnp.int32, (64, 64), 1)
-    rank = jnp.dot(
-        jnp.broadcast_to(mine, (8, 64)), (row < col).astype(F32), precision=HIGHEST, preferred_element_type=F32
-    )
-    slot = lax.broadcasted_iota(jnp.int32, (8, 64), 0).astype(F32)
-    picked = jnp.where(rank == slot, mine, 0.0)
-    chosen = [
-        jnp.dot(picked, rows_of[n], precision=HIGHEST, preferred_element_type=F32) for n in range(STEPS)
-    ]
+    chosen = choose(last)
     for s in range(SLOTS):
         for k in range(2 * NF // 8):
-            total = spread[0, 8 * k:8 * k + 8] * chosen[0][s:s + 1]
-            for n in range(1, STEPS):
-                total += spread[n, 8 * k:8 * k + 8] * chosen[n][s:s + 1]
-            out_s[0, 0, 0, s, 8 * k:8 * k + 8] = total
+            out_s[0, 0, 0, s, 8 * k:8 * k + 8] += spread[last, 8 * k:8 * k + 8] * chosen[s:s + 1]
 
     total = part[me // 4]
     for k in range(1, NGY * NAF):
@@ -467,10 +501,15 @@
     for copy in sends:
         copy.wait()
 
+    @pl.when(is_holder)
+    def _():
+        for k, device in enumerate(receivers):
+            sample_copy(last, k, device).wait_send()
+
     @pl.when(is_relay)
     def _():
         for k in range(ROW - 1):
-            relay_copy(STEPS - 1, k).wait_send()
+            relay_copy(last, k).wait_send()
 
 
 def on_device(constants, fields, polarization, material, eps_inf, pole_strength, pole_freq, damping, owner):
@@ -502,6 +541,7 @@
             pltpu.VMEM((2, BZ, 2 * NANG), F32),
             pltpu.VMEM((2, 2, BY, NANG), F32),
             pltpu.VMEM((STEPS, 2 * NF, 128), F32),
+            pltpu.VMEM((2, 128, 128), F32),
             pltpu.VMEM((2, 8, 128), F32),
             pltpu.VMEM((8, 8, 128), F32),
             dma(8), dma(5), dma(5), dma(7), dma(2, 7), dma(3), dma(3),

time: 62 us -> 58.5 us (0.944)
  Pallas kernels: 57.7 us -> 54.1 us
    pallas_call x1, Pallas kernels: 57.7 us -> 54.1 us  [on_device(): pl.pallas_call(kernel, out_shape=(pltpu.VMEM(fields.shape, F32), pltpu.VM...]
where the time goes in v4:
time: 58.5 us; the launch traced here: 58.3 us
  Pallas kernels  54.1 us (92%)
  local copies, waits for them, and re-layouts  3.58 us (6%)
  between operations  0.64 us (1%)
    pallas_call x1, Pallas kernels, on_device(): pl.pallas_call(kernel, out_shape=(pltpu.VMEM(fields.shape, F32), pltpu.VM...  54.1 us
    unnamed x4, local copies, waits for them, and re-layouts  3.58 us

profile of v4, /device:TPU:1, one launch (start us, length us, event | category | flops | bytes accessed | tf_op | source)
XLA Modules:
  0.0 58.3 jit_solution(1827096329763852478)
XLA Ops:
  0.6 54.1 %fdtd.1 = (f32[6,32,16,128]{3,2,1,0:T(8,128)S(1)}, f32[2,3,32,16,128]{4,3,2,1,0:T(8,128)S(1)}, f32[1,1,1,8,64,128]{5,4,3,2,1,0:T(8,128)S(1)}, f32[8,32]{1,0:T(8,128)S(1)}) custom-call(f32[4]{0:T(128)} %eps_ref.1, f32[4]{0:T(128)} %strength_ref.1, f32[4]{0:T(128)} %freq_ref.1, f32[4]{0:T(128)} %damp_ref.1, f32[8,64]{1,0:T(8,128)} %constant.8.clone.weight_ref, ...), custom_call_target="tpu_custom_call" | custom-call | tf_op jit(solution)/shard_map/fdtd/pallas_call | solution.py:521
  54.8 1.1 %copy.20 = f32[6,32,16,128]{3,2,1,0:T(8,128)} copy(f32[6,32,16,128]{3,2,1,0:T(8,128)S(1)} %get-tuple-element.4) | data formatting | bytes 3145728
  55.9 0.6 %copy.23 = f32[8,32]{1,0:T(8,128)} copy(f32[8,32]{1,0:T(8,128)S(1)} %get-tuple-element.7) | data formatting | bytes 2048
  56.5 0.7 %copy.22 = f32[1,1,1,8,64,128]{5,4,3,2,1,0:T(8,128)} copy(f32[1,1,1,8,64,128]{5,4,3,2,1,0:T(8,128)S(1)} %get-tuple-element.6) | data formatting | bytes 524288
  57.2 1.1 %copy.21 = f32[2,3,32,16,128]{4,3,2,1,0:T(8,128)} copy(f32[2,3,32,16,128]{4,3,2,1,0:T(8,128)S(1)} %get-tuple-element.5) | data formatting | bytes 3145728

commit v5 on v4

--- a/solution.py
+++ b/solution.py
@@ -75,7 +75,7 @@
     is_holder = jnp.logical_and(gx == NGX - 1, c == 1)
     row_end = gx // ROW * ROW + ROW - 1
     is_last_row = gx // ROW == NGX // ROW - 1
-    is_relay = jnp.logical_and(gx == row_end, jnp.logical_not(is_last_row))
+    is_relay = jnp.logical_and(jnp.logical_and(gx == row_end, c == 1), jnp.logical_not(is_last_row))
     fed_by_relay = jnp.logical_and(gx != row_end, jnp.logical_not(is_last_row))
     fed_by_holder = jnp.logical_or(is_relay, jnp.logical_and(is_last_row, gx != row_end))
     me = gy * NAF + c
@@ -101,7 +101,7 @@
 
     @pl.when(fed_by_relay)
     def _():
-        greet((row_end, gy, c))
+        greet((row_end, gy, 1))
 
     @pl.when(fed_by_holder)
     def _():
@@ -143,8 +143,8 @@
         NGY * NAF - 1
         + across_up.astype(jnp.int32) + across_down.astype(jnp.int32)
         + across_up_left.astype(jnp.int32) + across_down_right.astype(jnp.int32)
-        + jnp.where(is_holder, 2 * (NGX // ROW + ROW - 2), 0)
-        + jnp.where(is_relay, ROW - 1, 0)
+        + jnp.where(is_holder, NGX // ROW - 1 + 2 * (ROW - 1), 0)
+        + jnp.where(is_relay, 2 * (ROW - 1), 0)
     )
     pl.semaphore_wait(barrier, count)
 
@@ -302,34 +302,38 @@
                 old_ref[d, z, i - 1, s] = new
                 e_new[d, z, i, r] = value + inverse * (DT * curl[d] - (new - now))
 
-    def sample_copy(n, k, device):
-        g, t = device
+    def sample_copy(n, k, g, t):
         return pltpu.make_async_remote_copy(
             src_ref=stage.at[n, t], dst_ref=samp.at[n], send_sem=samp_send.at[k], recv_sem=samp_recv.at[n],
             device_id=(g, gy, t), device_id_type=MESH,
         )
 
-    receivers = [(NGX - 1, 0)]
-    receivers += [(ROW * k + ROW - 1, t) for k in range(NGX // ROW - 1) for t in range(2)]
-    receivers += [(NGX - ROW + k, t) for k in range(ROW - 1) for t in range(2)]
+    def row_copies(n):
+        return [
+            sample_copy(n, 2 * k + t, row_end - 1 - lax.rem(k + 1, ROW - 1), t) for k in range(ROW - 1) for t in range(2)
+        ] + [sample_copy(n, 2 * ROW - 2, row_end, 0)]
 
     def relay_copy(n, k):
         return pltpu.make_async_remote_copy(
-            src_ref=samp.at[n], dst_ref=samp.at[n], send_sem=samp_send.at[k], recv_sem=samp_recv.at[n],
-            device_id=(row_end - 1 - k, gy, c), device_id_type=MESH,
+            src_ref=stage.at[n], dst_ref=stage.at[n], send_sem=samp_send.at[2 * ROW - 1 + k],
+            recv_sem=samp_recv.at[n], device_id=(ROW * k + ROW - 1, gy, 1), device_id_type=MESH,
         )
+
+    def relay_copies(n):
+        return [relay_copy(n, k) for k in range(NGX // ROW - 1)]
 
     def relay(n):
         @pl.when(is_relay)
         def _():
             @pl.when(n > 0)
             def _():
-                for k in range(ROW - 1):
-                    relay_copy(n - 1, k).wait_send()
+                for copy in row_copies(n - 1):
+                    copy.wait_send()
 
             relay_copy(n, 0).wait_recv()
-            for k in range(ROW - 1):
-                relay_copy(n, k).start()
+            for copy in row_copies(n):
+                copy.start()
+            samp[n] = stage[n, 1]
 
     def start_next(n, p):
         @pl.when(n < STEPS - 1)
@@ -383,15 +387,15 @@
         def _():
             @pl.when(n > 0)
             def _():
-                for k, device in enumerate(receivers):
-                    sample_copy(n - 1, k, device).wait_send()
+                for copy in relay_copies(n - 1) + row_copies(n - 1):
+                    copy.wait_send()
 
             for t in range(2):
                 for d in range(2):
                     stage[n, t, d] = e_new[d + 1, t, 1, 8:24]
                     stage[n, t, d + 2] = H[d + 1, t, 1, 8:24]
-            for k, device in enumerate(receivers):
-                sample_copy(n, k, device).start()
+            for copy in relay_copies(n) + row_copies(n):
+                copy.start()
             samp[n] = stage[n, 1]
 
     @pl.loop(0, STEPS // 2)
@@ -412,16 +416,25 @@
         ))
         s, d = out(c)
         sends.append(pltpu.make_async_copy(s, d, out_sem.at[k]))
-    for copy in sends:
-        copy.start()
+    @pl.when(jnp.logical_not(is_relay))
+    def _():
+        for copy in sends:
+            copy.start()
 
     last = STEPS - 1
+    relay(last)
+
+    @pl.when(is_relay)
+    def _():
+        for copy in sends:
+            copy.start()
+
     is_end = jnp.logical_not(jnp.logical_or(is_holder, is_relay))
 
     @pl.when(is_end)
     def _():
         for n in range(last):
-            sample_copy(n, 0, (0, 0)).wait_recv()
+            sample_copy(n, 0, 0, 0).wait_recv()
 
     def sample(n):
         return samp[n].reshape(4 * BY, 128)
@@ -456,11 +469,9 @@
                 total += spread[n, 8 * k:8 * k + 8] * chosen[n][s:s + 1]
             out_s[0, 0, 0, s, 8 * k:8 * k + 8] = total
 
-    relay(last)
-
     @pl.when(is_end)
     def _():
-        sample_copy(last, 0, (0, 0)).wait_recv()
+        sample_copy(last, 0, 0, 0).wait_recv()
 
     for f in range(2):
         for k in range(2):
@@ -503,13 +514,23 @@
 
     @pl.when(is_holder)
     def _():
-        for k, device in enumerate(receivers):
-            sample_copy(last, k, device).wait_send()
+        for copy in relay_copies(last) + row_copies(last):
+            copy.wait_send()
 
     @pl.when(is_relay)
     def _():
-        for k in range(ROW - 1):
-            relay_copy(last, k).wait_send()
+        for copy in row_copies(last):
+            copy.wait_send()
+
+
+def write_out(*refs):
+    count = len(refs) // 2
+    sem = refs[-1]
+    copies = [pltpu.make_async_copy(refs[i], refs[count + i], sem.at[i]) for i in range(count)]
+    for copy in copies:
+        copy.start()
+    for copy in copies:
+        copy.wait()
 
 
 def on_device(constants, fields, polarization, material, eps_inf, pole_strength, pole_freq, damping, owner):
@@ -518,13 +539,11 @@
     vmem = pl.BlockSpec(memory_space=pltpu.VMEM)
     hbm = pl.BlockSpec(memory_space=pl.ANY)
     dma = lambda *shape: pltpu.SemaphoreType.DMA(shape)
-    return pl.pallas_call(
+    shapes = (fields.shape, polarization.shape, (1, 1, 1, SLOTS, 2 * NF, BZ), (8, 32))
+    results = pl.pallas_call(
         kernel,
         out_shape=(
-            pltpu.VMEM(fields.shape, F32),
-            pltpu.VMEM(polarization.shape, F32),
-            pltpu.VMEM((1, 1, 1, SLOTS, 2 * NF, BZ), F32),
-            pltpu.VMEM((8, 32), F32),
+            *(pltpu.VMEM(shape, F32) for shape in shapes),
         ),
         in_specs=[smem] * 5 + [vmem] + [hbm] * 6,
         out_specs=(vmem, vmem, vmem, vmem),
@@ -545,7 +564,7 @@
             pltpu.VMEM((2, 8, 128), F32),
             pltpu.VMEM((8, 8, 128), F32),
             dma(8), dma(5), dma(5), dma(7), dma(2, 7), dma(3), dma(3),
-            dma(13), dma(STEPS), dma(8), dma(8), dma(4), dma(4), dma(4),
+            dma(2 * ROW + 2), dma(STEPS), dma(8), dma(8), dma(4), dma(4), dma(4),
         ],
         compiler_params=pltpu.CompilerParams(
             collective_id=0, has_side_effects=True, vmem_limit_bytes=56 << 20
@@ -555,6 +574,14 @@
         eps_inf, pole_strength, pole_freq, damping, weights, owner.reshape(1, 64),
         fields, polarization, material, spread, z_table, y_table,
     )
+    return pl.pallas_call(
+        write_out,
+        out_shape=tuple(jax.ShapeDtypeStruct(shape, F32) for shape in shapes),
+        in_specs=[vmem] * 4,
+        out_specs=[hbm] * 4,
+        scratch_shapes=[dma(4)],
+        name="write_out",
+    )(*(pltpu.with_memory_space_constraint(x, pltpu.VMEM) for x in results))
 
 
 def solution(mesh):

time: 58.5 us -> 56.1 us (0.959)
  local copies, waits for them, and re-layouts: 3.58 us -> 0 us
  Pallas kernels: 54.1 us -> 55.3 us
    unnamed x4 -> x0, local copies, waits for them, and re-layouts: 3.58 us -> none
    pallas_call x1 -> x2, Pallas kernels: 54.1 us -> 55.3 us  [the longest x1 53.5 us: on_device(): pl.pallas_call(kernel, out_shape=(*(pltpu.VMEM(shape, F32) for shape in s...]
where the time goes in v5:
time: 56.1 us; the launch traced here: 56 us
  Pallas kernels  55.3 us (99%)
  between operations  0.64 us (1%)
    pallas_call x1, Pallas kernels, on_device(): pl.pallas_call(kernel, out_shape=(*(pltpu.VMEM(shape, F32) for shape in s...  53.5 us
    pallas_call x1, Pallas kernels, on_device(): pl.pallas_call(write_out, out_shape=tuple((jax.ShapeDtypeStruct(shape, F3...  1.78 us

profile of v5, /device:TPU:1, one launch (start us, length us, event | category | flops | bytes accessed | tf_op | source)
XLA Modules:
  0.0 56.0 jit_solution(9641263072227751788)
XLA Ops:
  0.6 53.5 %fdtd.1 = (f32[6,32,16,128]{3,2,1,0:T(8,128)S(1)}, f32[2,3,32,16,128]{4,3,2,1,0:T(8,128)S(1)}, f32[1,1,1,8,64,128]{5,4,3,2,1,0:T(8,128)S(1)}, f32[8,32]{1,0:T(8,128)S(1)}) custom-call(f32[4]{0:T(128)} %eps_ref.1, f32[4]{0:T(128)} %strength_ref.1, f32[4]{0:T(128)} %freq_ref.1, f32[4]{0:T(128)} %damp_ref.1, f32[8,64]{1,0:T(8,128)} %constant.8.clone.weight_ref, ...), custom_call_target="tpu_custom_call" | custom-call | tf_op jit(solution)/shard_map/fdtd/pallas_call | solution.py:543
  54.2 1.8 %write_out.1 = (f32[6,32,16,128]{3,2,1,0:T(8,128)}, f32[2,3,32,16,128]{4,3,2,1,0:T(8,128)}, f32[1,1,1,8,64,128]{5,4,3,2,1,0:T(8,128)}, f32[8,32]{1,0:T(8,128)}) custom-call(f32[6,32,16,128]{3,2,1,0:T(8,128)S(1)} %get-tuple-element.8.refs_0_, f32[2,3,32,16,128]{4,3,2,1,0:T(8,128)S(1)} %get-tuple-element.9.refs_1_, ...), custom_call_target="tpu_custom_call" | custom-call | tf_op jit(solution)/shard_map/write_out/pallas_call | solution.py:577

commit v6 on v5

--- a/solution.py
+++ b/solution.py
@@ -61,16 +61,19 @@
     samp_send, samp_recv, far_send, far_recv, out_sem, out_send, out_recv,
 ):
     gx, gy, c = lax.axis_index("gx"), lax.axis_index("gy"), lax.axis_index("af")
-    place = 2 * gx + c
+    half = lax.rem(gx + c + 1, 2)
+    place = 2 * gx + half
     E = (E0, E1)
     other = 1 - c
     has_up, has_down = place < 2 * NGX - 1, place > 0
     has_right, has_left = gy < NGY - 1, gy > 0
-    up = (gx + c, gy, other)
-    down = (gx - other, gy, other)
+    up_core = jnp.where(half == 1, c, other)
+    down_core = jnp.where(half == 1, other, c)
+    up = (gx + half, gy, up_core)
+    down = (gx - (1 - half), gy, down_core)
     right, left = (gx, gy + 1, c), (gx, gy - 1, c)
-    up_left = (gx + c, gy - 1, other)
-    down_right = (gx - other, gy + 1, other)
+    up_left = (gx + half, gy - 1, up_core)
+    down_right = (gx - (1 - half), gy + 1, down_core)
     partner = (gx, gy, other)
     is_holder = jnp.logical_and(gx == NGX - 1, c == 1)
     row_end = gx // ROW * ROW + ROW - 1
@@ -88,8 +91,8 @@
     for k in range(1, NGY * NAF):
         them = lax.rem(me + k, NGY * NAF)
         greet((gx, them // NAF, lax.rem(them, NAF)))
-    across_up = jnp.logical_and(c == 1, has_up)
-    across_down = jnp.logical_and(c == 0, has_down)
+    across_up = jnp.logical_and(half == 1, has_up)
+    across_down = jnp.logical_and(half == 0, has_down)
     across_up_left = jnp.logical_and(across_up, has_left)
     across_down_right = jnp.logical_and(across_down, has_right)
     for there, device in (
@@ -107,8 +110,8 @@
     def _():
         greet((NGX - 1, gy, 1))
 
-    here = pl.ds(c * HX, HX)
-    there = pl.ds(other * HX, HX)
+    here = pl.ds(half * HX, HX)
+    there = pl.ds((1 - half) * HX, HX)
     loads = [
         (fields_ref.at[0:3, here], E0.at[:, c, 1:HX + 1, 8:24]),
         (fields_ref.at[3:6, here], H.at[:, c, 1:HX + 1, 8:24]),
@@ -310,7 +313,7 @@
 
     def row_copies(n):
         return [
-            sample_copy(n, 2 * k + t, row_end - 1 - lax.rem(k + 1, ROW - 1), t) for k in range(ROW - 1) for t in range(2)
+            sample_copy(n, 2 * k + t, row_end - ROW + 1 + k, t) for k in range(ROW - 1) for t in range(2)
         ] + [sample_copy(n, 2 * ROW - 2, row_end, 0)]
 
     def relay_copy(n, k):
@@ -355,17 +358,12 @@
 
         finish(along_y)
 
-        @pl.loop(0, 3)
-        def _(b):
-            for u in range(5):
-                magnetic(e, 1 + 5 * b + u, 0, has_left)
-                magnetic(e, 1 + 5 * b + u, 2)
-
-        @pl.loop(0, 2)
-        def _(b):
-            for u in range(7):
-                electric(e, e_new, now_ref, old_ref, 2 + 7 * b + u, 1)
-                electric(e, e_new, now_ref, old_ref, 2 + 7 * b + u, 2)
+        for i in range(1, HX):
+            magnetic(e, i, 0, has_left)
+            magnetic(e, i, 2)
+        for i in range(2, HX):
+            electric(e, e_new, now_ref, old_ref, i, 1)
+            electric(e, e_new, now_ref, old_ref, i, 2)
 
         finish(along_x)
         magnetic(e, 0, 1, has_down)

time: 56.1 us -> 54.4 us (0.970)
  Pallas kernels: 55.3 us -> 53.6 us
    pallas_call x1, Pallas kernels: 53.5 us -> 51.8 us  [on_device(): pl.pallas_call(kernel, out_shape=(*(pltpu.VMEM(shape, F32) for shape in s...]
where the time goes in v6:
time: 54.4 us; the launch traced here: 54.2 us
  Pallas kernels  53.6 us (99%)
  between operations  0.64 us (1%)
    pallas_call x1, Pallas kernels, on_device(): pl.pallas_call(kernel, out_shape=(*(pltpu.VMEM(shape, F32) for shape in s...  51.8 us
    pallas_call x1, Pallas kernels, on_device(): pl.pallas_call(write_out, out_shape=tuple((jax.ShapeDtypeStruct(shape, F3...  1.78 us

profile of v6, /device:TPU:1, one launch (start us, length us, event | category | flops | bytes accessed | tf_op | source)
XLA Modules:
  0.0 54.2 jit_solution(5868508529634269853)
XLA Ops:
  0.6 51.8 %fdtd.1 = (f32[6,32,16,128]{3,2,1,0:T(8,128)S(1)}, f32[2,3,32,16,128]{4,3,2,1,0:T(8,128)S(1)}, f32[1,1,1,8,64,128]{5,4,3,2,1,0:T(8,128)S(1)}, f32[8,32]{1,0:T(8,128)S(1)}) custom-call(f32[4]{0:T(128)} %eps_ref.1, f32[4]{0:T(128)} %strength_ref.1, f32[4]{0:T(128)} %freq_ref.1, f32[4]{0:T(128)} %damp_ref.1, f32[8,64]{1,0:T(8,128)} %constant.8.clone.weight_ref, ...), custom_call_target="tpu_custom_call" | custom-call | tf_op jit(solution)/shard_map/fdtd/pallas_call | solution.py:541
  52.5 1.8 %write_out.1 = (f32[6,32,16,128]{3,2,1,0:T(8,128)}, f32[2,3,32,16,128]{4,3,2,1,0:T(8,128)}, f32[1,1,1,8,64,128]{5,4,3,2,1,0:T(8,128)}, f32[8,32]{1,0:T(8,128)}) custom-call(f32[6,32,16,128]{3,2,1,0:T(8,128)S(1)} %get-tuple-element.8.refs_0_, f32[2,3,32,16,128]{4,3,2,1,0:T(8,128)S(1)} %get-tuple-element.9.refs_1_, ...), custom_call_target="tpu_custom_call" | custom-call | tf_op jit(solution)/shard_map/write_out/pallas_call | solution.py:575
